TPU v7x, 768 devices: a whole 4x8x12 slice. The times are simulated.
768 devices in a mesh: blk: 192 (over y, z, core), mpo: 4 (over x).
Axes of the slice: x: 4, y: 8, z: 12, core: 2. Of those that a mesh axis runs over, the one named last changes fastest.
Arguments:
- psi: bfloat16 [768, 256, 256], P('blk'), may hold values from -6 to 6
- sector_class: int32 [768], P('blk'), may hold values from 1 to 4
- left_env: bfloat16 [12288, 256, 256], P(('blk', 'mpo')), may hold values from -0.375 to 0.375
- right_env: bfloat16 [12288, 256, 256], P(('blk', 'mpo')), may hold values from -0.375 to 0.375
- term_source: int32 [12288], P(('blk', 'mpo')), may hold values from 0 to 767, as said below
- term_target: int32 [12288], P(('blk', 'mpo')), may hold values from -1 to 3, as said below
Outputs:
- hpsi: float32 [768, 256, 256], P('blk', 'mpo')
Inputs may be any that keep to these rules, and one draw needn't show every extreme that they name: `term_source`: slot t of owner b reads a sector within 4 sectors of the owner's own: between (b - 1) * 4 and (b + 2) * 4 - 1. `term_target`: every device has at least 8 live slots, and some device has all 16 slots live.
All inputs are finite; a program needn't handle non-finite values.
Results may differ from a plain program's by a relative error of at most 0.0029.
Values may be sent and summed in bfloat16 or wider, within the bound.
No kernel may reach another device: no remote copies, remote signals or barrier semaphores. Data moves between devices by JAX's collectives and lax.ppermute only.
A program may use at most 32 MiB of HBM per device.

v0:
```python
import jax
import jax.numpy as jnp
from jax import lax
from jax.sharding import PartitionSpec as P


def extended(block, sides, width):
    for axis, dim in sides:
        count = lax.axis_size(axis)
        forward = [(i, i + 1) for i in range(count - 1)]
        backward = [(target, source) for source, target in forward]
        low = lax.ppermute(
            lax.slice_in_dim(block, block.shape[dim] - width, None, axis=dim), axis, forward
        )
        high = lax.ppermute(lax.slice_in_dim(block, 0, width, axis=dim), axis, backward)
        block = jnp.concatenate([low, block, high], axis=dim)
    return block


def body(psi, sector_class, left_env, right_env, term_source, term_target):
    sectors = psi.shape[0]
    block_size = psi.shape[1]
    groups = lax.axis_size("mpo")
    part_rows = block_size // groups
    position = lax.axis_index("mpo")
    owner_index = lax.axis_index("blk")
    row_index = jnp.arange(block_size, dtype=jnp.int32)
    live_rows = sector_class * (block_size // 4)
    col_keep = row_index[None, None, :] < live_rows[:, None, None]
    keep_mask = (row_index[None, :, None] < live_rows[:, None, None]) & col_keep
    masked = jnp.where(keep_mask, psi, jnp.zeros_like(psi))
    window = extended(masked, (("blk", 0),), sectors)
    local_index = term_source - (owner_index - 1) * sectors
    picked = jnp.take(window, local_index, axis=0)
    left_product = jnp.einsum(
        "tij,tjk->tik", left_env, picked, preferred_element_type=jnp.float32
    ).astype(jnp.bfloat16)
    second = jnp.einsum("tik,tlk->til", left_product, right_env, preferred_element_type=jnp.float32)
    onehot = (term_target[None, :] == jnp.arange(sectors, dtype=jnp.int32)[:, None]).astype(
        jnp.float32
    )
    partial_value = jnp.einsum("pt,til->pil", onehot, second, precision=lax.Precision.HIGHEST)
    summed = lax.psum_scatter(partial_value, "mpo", scatter_dimension=1, tiled=True)
    out_rows = position * part_rows + jnp.arange(part_rows, dtype=jnp.int32)
    keep_out = (out_rows[None, :, None] < live_rows[:, None, None]) & col_keep
    return jnp.where(keep_out, summed, jnp.zeros_like(summed))


def solution(mesh):
    placed = (
        P("blk", None, None),
        P("blk"),
        P(("blk", "mpo"), None, None),
        P(("blk", "mpo"), None, None),
        P(("blk", "mpo")),
        P(("blk", "mpo")),
    )
    return jax.shard_map(
        body, mesh=mesh, in_specs=placed, out_specs=P("blk", "mpo", None), check_vma=False
    )
```

profile of v0, /device:TPU:56, one launch (start us, length us, event | category | flops | bytes accessed | tf_op | source)
XLA Modules:
  0.0 118.8 jit_solution(1062379704730967578)
XLA Ops:
  6.5 0.0 copy-start
  6.5 0.0 all-reduce.3.cloned.1.call-start
  6.5 0.8 broadcast_multiply_fusion
  7.3 0.1 iota_compare_fusion
  7.4 1.3 %and_select_fusion = bf16[4,256,256]{2,1,0:T(8,128)(2,1)S(1)} fusion(bf16[4,256,256]{2,1,0:T(8,128)(2,1)} %param.6, pred[4,256]{1,0:T(4,128)(4,1)S(1)} %iota_compare_fusion), kind=kLoop, calls=%fused_computation.10 | loop fusion | flops 524288 | bytes 1049600 | tf_op jit(solution)/shard_map/jit(_where)/select_n | solution.py:31
  8.7 1.9 %collective-permute-start = (bf16[4,256,256]{2,1,0:T(8,128)(2,1)S(1)}, bf16[4,256,256]{2,1,0:T(8,128)(2,1)S(1)}, u32[]{:S(2)}, u32[]{:S(2)}) collective-permute-start(bf16[4,256,256]{2,1,0:T(8,128)(2,1)S(1)} %and_select_fusion), channel_id=1, source_target_pairs={{0,4},{4,8},{8,12},{12,16},{16,20},{20,24},{24,28},{28,32},{32,36}... | collective-permute-start | bytes 1572872 | tf_op jit(solution)/shard_map/ppermute | solution.py:12
  10.6 14.8 %collective-permute-start.1 = (bf16[4,256,256]{2,1,0:T(8,128)(2,1)S(1)}, bf16[4,256,256]{2,1,0:T(8,128)(2,1)}, u32[]{:S(2)}, u32[]{:S(2)}) collective-permute-start(bf16[4,256,256]{2,1,0:T(8,128)(2,1)S(1)} %and_select_fusion), channel_id=1, source_target_pairs={{4,0},{8,4},{12,8},{16,12},{20,16},{24,20},{28,24},{32,28},{36,32}... | collective-permute-start | bytes 1572872 | tf_op jit(solution)/shard_map/ppermute | solution.py:15
  25.5 0.7 compare_and_fusion
  26.1 4.2 %collective-permute-done = bf16[4,256,256]{2,1,0:T(8,128)(2,1)S(1)} collective-permute-done((bf16[4,256,256]{2,1,0:T(8,128)(2,1)S(1)}, bf16[4,256,256]{2,1,0:T(8,128)(2,1)S(1)}, u32[]{:S(2)}, u32[]{:S(2)}) %collective-permute-start) | collective-permute-done | bytes 524320 | tf_op jit(solution)/shard_map/ppermute | solution.py:12
  30.4 1.8 %collective-permute-done.1 = bf16[4,256,256]{2,1,0:T(8,128)(2,1)} collective-permute-done((bf16[4,256,256]{2,1,0:T(8,128)(2,1)S(1)}, bf16[4,256,256]{2,1,0:T(8,128)(2,1)}, u32[]{:S(2)}, u32[]{:S(2)}) %collective-permute-start.1) | collective-permute-done | bytes 524320 | tf_op jit(solution)/shard_map/ppermute | solution.py:15
  32.1 2.4 %pad_maximum_fusion = bf16[12,256,256]{2,1,0:T(8,128)(2,1)} fusion(bf16[4,256,256]{2,1,0:T(8,128)(2,1)} %collective-permute-done.1, bf16[4,256,256]{2,1,0:T(8,128)(2,1)S(1)} %and_select_fusion, bf16[4,256,256]{2,1,0:T(8,128)(2,1)S(1)} %collective-permute-done), kind=kLoop, calls=%fused_computation.8 | loop fusion | flops 1572864 | bytes 3145728 | tf_op jit(solution)/shard_map/concatenate | solution.py:16
  34.5 3.4 %gather_fusion = bf16[16,256,256]{2,1,0:T(8,128)(2,1)} fusion(bf16[12,256,256]{2,1,0:T(8,128)(2,1)} %pad_maximum_fusion, s32[1024]{0:T(1024)S(1)} %pad_clamp_fusion), kind=kCustom, calls=%fused_computation | custom fusion | bytes 4194368 | tf_op jit(solution)/shard_map/jit(_take)/gather | solution.py:34
  37.9 0.0 copy-done
  37.9 0.0 copy-start.1
  37.9 5.6 %fusion.2 = f32[16,256,256]{2,1,0:T(8,128)} fusion(bf16[16,256,256]{2,1,0:T(8,128)(2,1)S(1)} %copy-done, bf16[16,256,256]{2,1,0:T(8,128)(2,1)} %param.8, bf16[16,256,256]{2,1,0:T(8,128)(2,1)} %gather_fusion, pred[16]{0:T(512)(128)(4,1)S(1)} %get-tuple-element.5), kind=kOutput, calls=%fused_computation.3 | convolution fusion | flops 1075838976 | bytes 10485776 | tf_op jit(solution)/shard_map/tik,tlk->til/dot_general | solution.py:38
  43.5 0.0 copy-done.1
  43.5 6.8 %fusion = f32[4,256,256]{2,0,1:T(4,128)} fusion(f32[16,256,256]{2,1,0:T(8,128)} %fusion.2, s32[16]{0:T(128)S(1)} %copy-done.1), kind=kOutput, calls=%fused_computation.1 | convolution fusion | flops 50331712 | bytes 5242944 | tf_op jit(solution)/shard_map/pt,til->pil/dot_general | solution.py:42
  50.3 0.0 all-reduce.3.cloned.1.call-update
  50.4 1.3 %dynamic-slice = u32[1]{0:T(128)} dynamic-slice(u32[768]{0:T(1024)} %constant.44, u32[]{:T(128)S(6)} %add.21), dynamic_slice_sizes={1} | dynamic-slice | bytes 12
  52.3 0.1 broadcast_compare_fusion
  52.4 57.8 %all-reduce.3.cloned.1.call-done = f32[4,256,256]{2,0,1:T(4,128)} async-done(((f32[4,256,256]{2,0,1:T(4,128)}), f32[4,256,256]{2,0,1:T(4,128)}) %all-reduce.3.cloned.1.call-update) | async-done | bytes 1048592
  110.1 1.1 dynamic-slice_select_fusion
  111.2 0.8 copy.8
  (2 shorter events, 0.0 us)
Async XLA Ops:
  6.5 31.4 %copy-start = (bf16[16,256,256]{2,1,0:T(8,128)(2,1)S(1)}, bf16[16,256,256]{2,1,0:T(8,128)(2,1)}, u32[]{:S(2)}) copy-start(bf16[16,256,256]{2,1,0:T(8,128)(2,1)} %param.9) | copy-start | bytes 6291460
  6.5 103.6 %all-reduce.3.cloned.1.call-start = ((), (), s32[]{:S(2)}) async-start(), calls=%async_computation | async-start | bytes 2097152
  8.7 21.7 %collective-permute-start = (bf16[4,256,256]{2,1,0:T(8,128)(2,1)S(1)}, bf16[4,256,256]{2,1,0:T(8,128)(2,1)S(1)}, u32[]{:S(2)}, u32[]{:S(2)}) collective-permute-start(bf16[4,256,256]{2,1,0:T(8,128)(2,1)S(1)} %and_select_fusion), channel_id=1, source_target_pairs={{0,4},{4,8},{8,12},{12,16},{16,20},{20,24},{24,28},{28,32},{32,36}... | collective-permute-start | bytes 1572872 | tf_op jit(solution)/shard_map/ppermute | solution.py:12
  10.6 21.5 %collective-permute-start.1 = (bf16[4,256,256]{2,1,0:T(8,128)(2,1)S(1)}, bf16[4,256,256]{2,1,0:T(8,128)(2,1)}, u32[]{:S(2)}, u32[]{:S(2)}) collective-permute-start(bf16[4,256,256]{2,1,0:T(8,128)(2,1)S(1)} %and_select_fusion), channel_id=1, source_target_pairs={{4,0},{8,4},{12,8},{16,12},{20,16},{24,20},{28,24},{32,28},{36,32}... | collective-permute-start | bytes 1572872 | tf_op jit(solution)/shard_map/ppermute | solution.py:15
  37.9 5.6 %copy-start.1 = (s32[16]{0:T(128)S(1)}, s32[16]{0:T(128)}, u32[]{:S(2)}) copy-start(s32[16]{0:T(128)} %param.11) | copy-start | bytes 196
Sparse Core Ops, SparseCore 0:
  50.5 59.6 all-reduce.2
where the time goes:
time: 120 us; the launch traced here: 119 us
  waiting for transfers between devices  63.8 us (53%)
  starting transfers between devices  16.7 us (14%)
  between operations  14.1 us (12%)
  matrix products  12.4 us (10%)
  other arithmetic  6.37 us (5%)
  local copies, waits for them, and re-layouts  5.44 us (5%)
    unnamed x2, waiting for transfers between devices  57.8 us
    ppermute x1, starting transfers between devices, extended(): lax.ppermute(lax.slice_in_dim(block, 0, width, axis=dim), axis, backward)  14.8 us
    dot_general x1, matrix products, body(): jnp.einsum('pt,til->pil', onehot, second, precision=lax.Precision.HIGHEST)  6.82 us
    dot_general x1, matrix products, body(): jnp.einsum('tik,tlk->til', left_product, right_env, preferred_element_typ...  5.59 us
    ppermute x1, waiting for transfers between devices, extended(): lax.ppermute(lax.slice_in_dim(block, block.shape[dim] - width, None, axis...  4.24 us
    gather x1, local copies, waits for them, and re-layouts, body(): picked = jnp.take(window, local_index, axis=0)  3.4 us
  transfers between devices with their start and end apart: 3, of which 3 were waited for; matrix products, arithmetic and copies ran while one was open for 2% of the time, Pallas kernels for 0%

commit v1 on v0

v1 whole, which is shorter than its diff:
```python
import jax
import jax.numpy as jnp
from jax import lax
from jax.experimental import pallas as pl
from jax.experimental.pallas import tpu as pltpu
from jax.sharding import PartitionSpec as P

SMEM = pl.BlockSpec(memory_space=pltpu.SMEM)
VMEM = pl.BlockSpec(memory_space=pltpu.VMEM)


def masked_block(block, live):
    rows = lax.broadcasted_iota(jnp.int32, block.shape, 0)
    cols = lax.broadcasted_iota(jnp.int32, block.shape, 1)
    return jnp.where((rows < live) & (cols < live), block, jnp.zeros_like(block))


def terms_kernel(
    source_ref, target_ref, own_class, pair_class, next_class,
    own_ref, pair_ref, next_ref, left_ref, right_ref, out_ref, window, total,
):
    slots, size, _ = left_ref.shape
    sectors = own_ref.shape[0]
    groups, _, part_rows, _ = out_ref.shape
    owner = lax.axis_index("blk")
    odd = lax.rem(owner, 2)
    quarter = size // 4
    for group, (classes, blocks) in enumerate(
        ((own_class, own_ref), (pair_class, pair_ref), (next_class, next_ref))
    ):
        for s in range(sectors):
            window[group * sectors + s] = masked_block(blocks[s], classes[s] * quarter)
    total[...] = jnp.zeros_like(total)
    for t in range(slots):
        offset = source_ref[t] - (owner - 1) * sectors
        side = offset // sectors
        group = jnp.where(side == 1, 0, jnp.where((side == 2) == (odd == 0), 1, 2))
        place = group * sectors + lax.rem(offset, sectors)
        product = jnp.dot(
            left_ref[t], window[place], preferred_element_type=jnp.float32
        ).astype(jnp.bfloat16)
        term = lax.dot_general(
            product, right_ref[t], (((1,), (1,)), ((), ())), preferred_element_type=jnp.float32
        )
        target = target_ref[t]
        total[jnp.where(target < 0, sectors, target)] += term
    for g in range(groups):
        for s in range(sectors):
            out_ref[g, s] = total[s, g * part_rows : (g + 1) * part_rows, :].astype(out_ref.dtype)


def sum_kernel(class_ref, parts_ref, out_ref):
    groups, sectors, part_rows, size = parts_ref.shape
    position = lax.axis_index("mpo")
    quarter = size // 4
    for s in range(sectors):
        live = class_ref[s] * quarter
        summed = parts_ref[0, s].astype(jnp.float32)
        for g in range(1, groups):
            summed += parts_ref[g, s].astype(jnp.float32)
        rows = position * part_rows + lax.broadcasted_iota(jnp.int32, summed.shape, 0)
        cols = lax.broadcasted_iota(jnp.int32, summed.shape, 1)
        out_ref[s] = jnp.where((rows < live) & (cols < live), summed, 0.0)


def body(psi, sector_class, left_env, right_env, term_source, term_target):
    sectors, size, _ = psi.shape
    slots = left_env.shape[0]
    owners = lax.axis_size("blk")
    groups = lax.axis_size("mpo")
    part_rows = size // groups
    same_chip = [(i, i ^ 1) for i in range(owners)]
    next_chip = [(i, (i - 1 if i % 2 == 0 else i + 1) % owners) for i in range(owners)]
    following = lax.ppermute(psi, "blk", next_chip)
    pair = lax.ppermute(psi, "blk", same_chip)
    next_class = lax.ppermute(sector_class, "blk", next_chip)
    pair_class = lax.ppermute(sector_class, "blk", same_chip)
    keep = lambda x: pltpu.with_memory_space_constraint(x, pltpu.VMEM)
    parts = pl.pallas_call(
        terms_kernel,
        out_shape=jax.ShapeDtypeStruct((groups, sectors, part_rows, size), jnp.bfloat16),
        in_specs=[SMEM] * 5 + [VMEM] * 5,
        out_specs=VMEM,
        scratch_shapes=[
            pltpu.VMEM((3 * sectors, size, size), jnp.bfloat16),
            pltpu.VMEM((sectors + 1, size, size), jnp.float32),
        ],
        compiler_params=pltpu.CompilerParams(vmem_limit_bytes=24 * 2**20),
        cost_estimate=pl.CostEstimate(
            flops=4 * slots * size**3, bytes_accessed=4 * slots * size**2, transcendentals=0
        ),
        name="terms",
    )(
        term_source, term_target, sector_class, pair_class, next_class,
        keep(psi), keep(pair), keep(following), keep(left_env), keep(right_env),
    )
    received = lax.all_to_all(parts, "mpo", 0, 0)
    return pl.pallas_call(
        sum_kernel,
        out_shape=jax.ShapeDtypeStruct((sectors, part_rows, size), jnp.float32),
        in_specs=[SMEM, VMEM],
        out_specs=VMEM,
        name="sums",
    )(sector_class, received)


def solution(mesh):
    placed = (
        P("blk", None, None),
        P("blk"),
        P(("blk", "mpo"), None, None),
        P(("blk", "mpo"), None, None),
        P(("blk", "mpo")),
        P(("blk", "mpo")),
    )
    return jax.shard_map(
        body, mesh=mesh, in_specs=placed, out_specs=P("blk", "mpo", None), check_vma=False
    )
```

time: 120 us -> 50.4 us (0.42)
  the two profiles are of different devices: /device:TPU:56 before, /device:TPU:2 now
where the time goes in v1:
time: 50.4 us; the launch traced here: 50 us
  starting transfers between devices  23.3 us (46%)
  blocking collectives  11.4 us (23%)
  local copies, waits for them, and re-layouts  6.18 us (12%)
  Pallas kernels  4.55 us (9%)
  waiting for transfers between devices  4.46 us (9%)
    ppermute x1, starting transfers between devices, body(): following = lax.ppermute(psi, 'blk', next_chip)  17.6 us
    all_to_all x1, blocking collectives, body(): received = lax.all_to_all(parts, 'mpo', 0, 0)  11.4 us
    unnamed x12, local copies, waits for them, and re-layouts  6.18 us
    ppermute x1, waiting for transfers between devices, body(): next_class = lax.ppermute(sector_class, 'blk', next_chip)  4.45 us
    pallas_call x1, Pallas kernels, body(): pl.pallas_call(terms_kernel, out_shape=jax.ShapeDtypeStruct((groups, sect...  2.71 us
    ppermute x1, starting transfers between devices, body(): next_class = lax.ppermute(sector_class, 'blk', next_chip)  1.92 us
    ppermute x1, starting transfers between devices, body(): pair_class = lax.ppermute(sector_class, 'blk', same_chip)  1.92 us
    ppermute x1, starting transfers between devices, body(): pair = lax.ppermute(psi, 'blk', same_chip)  1.91 us
  transfers between devices with their start and end apart: 4, of which 1 were waited for; matrix products, arithmetic and copies ran while one was open for 0% of the time, Pallas kernels for 0%

profile of v1, /device:TPU:2, one launch (start us, length us, event | category | flops | bytes accessed | tf_op | source)
XLA Modules:
  0.0 50.0 jit_solution(18428184777459517651)
XLA Ops:
  0.0 1.9 %collective-permute-start.2 = (bf16[4,256,256]{2,1,0:T(8,128)(2,1)}, bf16[4,256,256]{2,1,0:T(8,128)(2,1)S(1)}, u32[]{:S(2)}, u32[]{:S(2)}) collective-permute-start(bf16[4,256,256]{2,1,0:T(8,128)(2,1)} %own_ref.1), channel_id=1, source_target_pairs={{0,4},{4,0},{8,12},{12,8},{16,20},{20,16},{24,28},{28,24},{32,36},... | collective-permute-start | bytes 1572872 | tf_op jit(solution)/shard_map/ppermute | solution.py:75
  1.9 17.6 %collective-permute-start.3 = (bf16[4,256,256]{2,1,0:T(8,128)(2,1)}, bf16[4,256,256]{2,1,0:T(8,128)(2,1)S(1)}, u32[]{:S(2)}, u32[]{:S(2)}) collective-permute-start(bf16[4,256,256]{2,1,0:T(8,128)(2,1)} %own_ref.1), channel_id=1, source_target_pairs={{0,764},{4,8},{8,4},{12,16},{16,12},{20,24},{24,20},{28,32},{32,28... | collective-permute-start | bytes 1572872 | tf_op jit(solution)/shard_map/ppermute | solution.py:74
  19.5 1.9 %collective-permute-start.1 = (s32[4]{0:T(128)}, s32[4]{0:T(128)S(1)}, u32[]{:S(2)}, u32[]{:S(2)}) collective-permute-start(s32[4]{0:T(128)} %class_ref.1), channel_id=1, source_target_pairs={{0,764},{4,8},{8,4},{12,16},{16,12},{20,24},{24,20},{28,32},{32,28... | collective-permute-start | bytes 56 | tf_op jit(solution)/shard_map/ppermute | solution.py:76
  21.4 1.9 %collective-permute-start = (s32[4]{0:T(128)}, s32[4]{0:T(128)S(1)}, u32[]{:S(2)}, u32[]{:S(2)}) collective-permute-start(s32[4]{0:T(128)} %class_ref.1), channel_id=1, source_target_pairs={{0,4},{4,0},{8,12},{12,8},{16,20},{20,16},{24,28},{28,24},{32,36},... | collective-permute-start | bytes 56 | tf_op jit(solution)/shard_map/ppermute | solution.py:77
  23.4 4.5 %collective-permute-done.1.next_class = s32[4]{0:T(128)S(1)} collective-permute-done((s32[4]{0:T(128)}, s32[4]{0:T(128)S(1)}, u32[]{:S(2)}, u32[]{:S(2)}) %collective-permute-start.1) | collective-permute-done | bytes 48 | tf_op jit(solution)/shard_map/ppermute | solution.py:76
  27.8 0.0 collective-permute-done.pair_class
  27.8 0.0 collective-permute-done.2.pair_ref
  27.8 0.0 collective-permute-done.3.next_ref
  27.8 0.0 copy-start
  27.9 1.6 %copy-done = bf16[16,256,256]{2,1,0:T(8,128)(2,1)S(1)} copy-done((bf16[16,256,256]{2,1,0:T(8,128)(2,1)S(1)}, bf16[16,256,256]{2,1,0:T(8,128)(2,1)}, u32[]{:S(2)}) %copy-start) | copy-done | bytes 2097176
  29.4 0.0 copy-start.1
  29.4 1.6 %copy-done.1 = bf16[16,256,256]{2,1,0:T(8,128)(2,1)S(1)} copy-done((bf16[16,256,256]{2,1,0:T(8,128)(2,1)S(1)}, bf16[16,256,256]{2,1,0:T(8,128)(2,1)}, u32[]{:S(2)}) %copy-start.1) | copy-done | bytes 2097176
  31.0 0.0 copy-start.2
  31.0 1.0 %copy-done.2 = bf16[4,256,256]{2,1,0:T(8,128)(2,1)S(1)} copy-done((bf16[4,256,256]{2,1,0:T(8,128)(2,1)S(1)}, bf16[4,256,256]{2,1,0:T(8,128)(2,1)}, u32[]{:S(2)}) %copy-start.2) | copy-done | bytes 524312
  32.1 0.0 copy-start.3
  32.1 0.7 %copy-done.3 = s32[4]{0:T(128)S(1)} copy-done((s32[4]{0:T(128)S(1)}, s32[4]{0:T(128)}, u32[]{:S(2)}) %copy-start.3) | copy-done | bytes 40
  32.7 0.0 copy-start.4
  32.7 0.7 %copy-done.4 = s32[16]{0:T(128)S(1)} copy-done((s32[16]{0:T(128)S(1)}, s32[16]{0:T(128)}, u32[]{:S(2)}) %copy-start.4) | copy-done | bytes 88
  33.4 0.0 copy-start.5
  33.4 0.7 %copy-done.5 = s32[16]{0:T(128)S(1)} copy-done((s32[16]{0:T(128)S(1)}, s32[16]{0:T(128)}, u32[]{:S(2)}) %copy-start.5) | copy-done | bytes 88
  34.0 2.7 %terms.1 = bf16[4,4,64,256]{3,2,1,0:T(8,128)(2,1)S(1)} custom-call(s32[16]{0:T(128)S(1)} %copy-done.4, s32[16]{0:T(128)S(1)} %copy-done.5, s32[4]{0:T(128)S(1)} %copy-done.3, s32[4]{0:T(128)S(1)} %collective-permute-done.pair_class, s32[4]{0:T(128)S(1)} %collective-permute-done.1.next_class, bf16[4,256,256]{2,1,0:T(8,128)(2,1)S(1)} %copy-done.2, ...), custom_call_target="tpu_custom_call" | custom-call | flops 1073741824 | bytes 4194304 | tf_op jit(solution)/shard_map/terms/pallas_call | solution.py:79
  36.8 11.4 %all_to_all.5.parts_ref = bf16[4,4,64,256]{3,2,1,0:T(8,128)(2,1)} all-to-all(bf16[4,4,64,256]{3,2,1,0:T(8,128)(2,1)S(1)} %terms.1), channel_id=1, replica_groups=mesh['blk'=192,'mpo'=4] {'mpo'}, dimensions={0} | all-to-all | bytes 1048576 | tf_op jit(solution)/shard_map/all_to_all | solution.py:97
  48.1 1.8 %sums.1 = f32[4,64,256]{2,1,0:T(8,128)} custom-call(s32[4]{0:T(128)} %class_ref.1, bf16[4,4,64,256]{3,2,1,0:T(8,128)(2,1)} %all_to_all.5.parts_ref), custom_call_target="tpu_custom_call" | custom-call | tf_op jit(solution)/shard_map/sums/pallas_call | solution.py:98
Async XLA Ops:
  0.0 27.8 %collective-permute-start.2 = (bf16[4,256,256]{2,1,0:T(8,128)(2,1)}, bf16[4,256,256]{2,1,0:T(8,128)(2,1)S(1)}, u32[]{:S(2)}, u32[]{:S(2)}) collective-permute-start(bf16[4,256,256]{2,1,0:T(8,128)(2,1)} %own_ref.1), channel_id=1, source_target_pairs={{0,4},{4,0},{8,12},{12,8},{16,20},{20,16},{24,28},{28,24},{32,36},... | collective-permute-start | bytes 1572872 | tf_op jit(solution)/shard_map/ppermute | solution.py:75
  1.9 25.9 %collective-permute-start.3 = (bf16[4,256,256]{2,1,0:T(8,128)(2,1)}, bf16[4,256,256]{2,1,0:T(8,128)(2,1)S(1)}, u32[]{:S(2)}, u32[]{:S(2)}) collective-permute-start(bf16[4,256,256]{2,1,0:T(8,128)(2,1)} %own_ref.1), channel_id=1, source_target_pairs={{0,764},{4,8},{8,4},{12,16},{16,12},{20,24},{24,20},{28,32},{32,28... | collective-permute-start | bytes 1572872 | tf_op jit(solution)/shard_map/ppermute | solution.py:74
  19.5 8.3 %collective-permute-start.1 = (s32[4]{0:T(128)}, s32[4]{0:T(128)S(1)}, u32[]{:S(2)}, u32[]{:S(2)}) collective-permute-start(s32[4]{0:T(128)} %class_ref.1), channel_id=1, source_target_pairs={{0,764},{4,8},{8,4},{12,16},{16,12},{20,24},{24,20},{28,32},{32,28... | collective-permute-start | bytes 56 | tf_op jit(solution)/shard_map/ppermute | solution.py:76
  21.4 6.4 %collective-permute-start = (s32[4]{0:T(128)}, s32[4]{0:T(128)S(1)}, u32[]{:S(2)}, u32[]{:S(2)}) collective-permute-start(s32[4]{0:T(128)} %class_ref.1), channel_id=1, source_target_pairs={{0,4},{4,0},{8,12},{12,8},{16,20},{20,16},{24,28},{28,24},{32,36},... | collective-permute-start | bytes 56 | tf_op jit(solution)/shard_map/ppermute | solution.py:77
  27.8 1.6 %copy-start = (bf16[16,256,256]{2,1,0:T(8,128)(2,1)S(1)}, bf16[16,256,256]{2,1,0:T(8,128)(2,1)}, u32[]{:S(2)}) copy-start(bf16[16,256,256]{2,1,0:T(8,128)(2,1)} %left_ref.1) | copy-start | bytes 6291460
  29.4 1.6 %copy-start.1 = (bf16[16,256,256]{2,1,0:T(8,128)(2,1)S(1)}, bf16[16,256,256]{2,1,0:T(8,128)(2,1)}, u32[]{:S(2)}) copy-start(bf16[16,256,256]{2,1,0:T(8,128)(2,1)} %right_ref.1) | copy-start | bytes 6291460
  31.0 1.0 %copy-start.2 = (bf16[4,256,256]{2,1,0:T(8,128)(2,1)S(1)}, bf16[4,256,256]{2,1,0:T(8,128)(2,1)}, u32[]{:S(2)}) copy-start(bf16[4,256,256]{2,1,0:T(8,128)(2,1)} %own_ref.1) | copy-start | bytes 1572868
  32.1 0.7 %copy-start.3 = (s32[4]{0:T(128)S(1)}, s32[4]{0:T(128)}, u32[]{:S(2)}) copy-start(s32[4]{0:T(128)} %class_ref.1) | copy-start | bytes 52
  32.7 0.7 %copy-start.4 = (s32[16]{0:T(128)S(1)}, s32[16]{0:T(128)}, u32[]{:S(2)}) copy-start(s32[16]{0:T(128)} %source_ref.1) | copy-start | bytes 196
  33.4 0.7 %copy-start.5 = (s32[16]{0:T(128)S(1)}, s32[16]{0:T(128)}, u32[]{:S(2)}) copy-start(s32[16]{0:T(128)} %target_ref.1) | copy-start | bytes 196

commit v2 on v0

v2 whole, which is shorter than its diff:
```python
import jax
import jax.numpy as jnp
from jax import lax
from jax.experimental import pallas as pl
from jax.experimental.pallas import tpu as pltpu
from jax.sharding import PartitionSpec as P

SMEM = pl.BlockSpec(memory_space=pltpu.SMEM)
VMEM = pl.BlockSpec(memory_space=pltpu.VMEM)
ANY = pl.BlockSpec(memory_space=pl.ANY)
UNROLL = 4


def in_vmem(x):
    return pltpu.with_memory_space_constraint(x, pltpu.VMEM)


def in_hbm(x):
    return pltpu.with_memory_space_constraint(x, pltpu.HBM)


def in_smem(x):
    return pltpu.with_memory_space_constraint(x, pltpu.SMEM)


def live_entries(shape, first_row, live):
    rows = first_row + lax.broadcasted_iota(jnp.int32, shape, 0)
    cols = lax.broadcasted_iota(jnp.int32, shape, 1)
    return (rows < live) & (cols < live)


def mask_kernel(class_hbm, psi_hbm, out_ref, classes, psi, class_sem, psi_sems):
    sectors, size, _ = psi.shape
    quarter = size // 4
    load_class = pltpu.make_async_copy(class_hbm, classes, class_sem)
    load_class.start()
    loads = []
    for s in range(sectors):
        loads.append(pltpu.make_async_copy(psi_hbm.at[s], psi.at[s], psi_sems.at[s]))
        loads[s].start()
    load_class.wait()
    cols = lax.broadcasted_iota(jnp.int32, (quarter, size), 1)
    for s in range(sectors):
        loads[s].wait()
        for q in range(4):
            rows = slice(q * quarter, (q + 1) * quarter)
            live = jnp.where(q < classes[s], classes[s] * quarter, 0)
            out_ref[s, rows, :] = jnp.where(cols < live, psi[s, rows, :], 0.0).astype(psi.dtype)


def fill_queue(queue, chosen, source_ref, target_ref):
    slots = source_ref.shape[0]
    for t in range(slots):
        queue[t] = 0
    count = jnp.int32(0)
    for t in range(slots):
        take = jnp.logical_and(target_ref[t] >= 0, chosen(source_ref[t]))
        queue[count] = jnp.where(take, t, 0)
        count += take.astype(jnp.int32)
    queue[slots] = count


def add_terms(queue, block_of, target_ref, left_ref, right_ref, total):
    slots = left_ref.shape[0]
    sectors = total.shape[0] - 1
    count = queue[slots]

    def step(i, carry):
        for j in range(UNROLL):
            n = i * UNROLL + j
            t = queue[n]
            product = jnp.dot(
                left_ref[t], block_of(t), preferred_element_type=jnp.float32
            ).astype(jnp.bfloat16)
            term = lax.dot_general(
                product, right_ref[t], (((1,), (1,)), ((), ())), preferred_element_type=jnp.float32
            )
            total[jnp.where(n < count, target_ref[t], sectors)] += term
        return carry

    lax.fori_loop(0, (count + UNROLL - 1) // UNROLL, step, 0)


def own_kernel(
    class_hbm, source_hbm, target_hbm, left_hbm, right_hbm, own_ref,
    total, left_ref, right_ref, keep_ref, copy_ref, target_ref, place_ref, others,
    classes, source_ref, queue, small_sems, left_sems, right_sems,
):
    slots, size, _ = left_ref.shape
    sectors, part_rows, _ = keep_ref.shape
    first = lax.axis_index("blk") * sectors
    chip_first = lax.axis_index("blk") // 2 * 2 * sectors
    small = [
        pltpu.make_async_copy(a, b, small_sems.at[i])
        for i, (a, b) in enumerate(
            ((source_hbm, source_ref), (target_hbm, target_ref), (class_hbm, classes))
        )
    ]
    large = []
    for t in range(slots):
        large.append(pltpu.make_async_copy(left_hbm.at[t], left_ref.at[t], left_sems.at[t]))
        large.append(pltpu.make_async_copy(right_hbm.at[t], right_ref.at[t], right_sems.at[t]))
    for copy in small + large:
        copy.start()
    copy_ref[...] = own_ref[...]
    total[...] = jnp.zeros_like(total)
    for copy in small:
        copy.wait()
    first_row = lax.axis_index("mpo") * part_rows
    for s in range(sectors):
        keep_ref[s] = live_entries(
            (part_rows, size), first_row, classes[s] * (size // 4)
        ).astype(jnp.float32)

    def is_own(source):
        return jnp.logical_and(source >= first, source < first + sectors)

    fill_queue(queue, is_own, source_ref, target_ref)
    fill_queue(others, lambda source: jnp.logical_not(is_own(source)), source_ref, target_ref)
    for t in range(slots):
        source = source_ref[t]
        near = jnp.logical_and(source >= chip_first, source < chip_first + 2 * sectors)
        place_ref[t] = lax.rem(source, sectors) + jnp.where(near, 0, sectors)
    for copy in large:
        copy.wait()
    add_terms(
        queue, lambda t: own_ref[lax.rem(source_ref[t], sectors)], target_ref, left_ref, right_ref, total
    )


def other_kernel(
    place_ref, target_ref, others, pair_ref, next_ref, given, left_ref, right_ref,
    parts_ref, total, window,
):
    groups, sectors, part_rows, _ = parts_ref.shape
    total[...] = given[...]
    window[:sectors] = pair_ref[...]
    window[sectors:] = next_ref[...]
    add_terms(others, lambda t: window[place_ref[t]], target_ref, left_ref, right_ref, total)
    for g in range(groups):
        for s in range(sectors):
            parts_ref[g, s] = total[s, g * part_rows : (g + 1) * part_rows, :].astype(
                parts_ref.dtype
            )


def body(psi, sector_class, left_env, right_env, term_source, term_target):
    sectors, size, _ = psi.shape
    slots = left_env.shape[0]
    owners = lax.axis_size("blk")
    groups = lax.axis_size("mpo")
    part_rows = size // groups
    same_chip = [(i, i ^ 1) for i in range(owners)]
    next_chip = [(i, i - 1 if i % 2 == 0 else i + 1) for i in range(1, owners - 1)]
    DMA = pltpu.SemaphoreType.DMA
    masked = pl.pallas_call(
        mask_kernel,
        out_shape=pltpu.VMEM(psi.shape, psi.dtype),
        in_specs=[ANY, ANY],
        out_specs=VMEM,
        scratch_shapes=[
            pltpu.SMEM((sectors,), jnp.int32),
            pltpu.VMEM(psi.shape, psi.dtype),
            DMA,
            DMA((sectors,)),
        ],
        name="masked",
    )(in_hbm(sector_class), in_hbm(psi))
    following = lax.ppermute(masked, "blk", next_chip)
    total, left, right, keep, copied, target, place, others = pl.pallas_call(
        own_kernel,
        out_shape=(
            pltpu.VMEM((sectors + 1, size, size), jnp.float32),
            pltpu.VMEM(left_env.shape, left_env.dtype),
            pltpu.VMEM(right_env.shape, right_env.dtype),
            pltpu.VMEM((sectors, part_rows, size), jnp.float32),
            pltpu.VMEM(psi.shape, psi.dtype),
            pltpu.SMEM((slots,), jnp.int32), pltpu.SMEM((slots,), jnp.int32), pltpu.SMEM((slots + 1,), jnp.int32),
        ),
        in_specs=[ANY] * 5 + [VMEM],
        out_specs=(VMEM,) * 5 + (SMEM,) * 3,
        scratch_shapes=[
            pltpu.SMEM((sectors,), jnp.int32),
            pltpu.SMEM((slots,), jnp.int32),
            pltpu.SMEM((slots + 1,), jnp.int32),
            DMA((3,)), DMA((slots,)), DMA((slots,)),
        ],
        compiler_params=pltpu.CompilerParams(vmem_limit_bytes=24 * 2**20),
        cost_estimate=pl.CostEstimate(
            flops=3 * slots * size**3, bytes_accessed=4 * slots * size**2, transcendentals=0
        ),
        name="own_terms",
    )(
        in_hbm(sector_class), in_hbm(term_source), in_hbm(term_target), in_hbm(left_env),
        in_hbm(right_env), in_vmem(masked),
    )
    pair = lax.ppermute(copied, "blk", same_chip)
    parts = pl.pallas_call(
        other_kernel,
        out_shape=pltpu.VMEM((groups, sectors, part_rows, size), jnp.bfloat16),
        in_specs=[SMEM] * 3 + [VMEM] * 5,
        out_specs=VMEM,
        scratch_shapes=[
            pltpu.VMEM((sectors + 1, size, size), jnp.float32),
            pltpu.VMEM((2 * sectors, size, size), jnp.bfloat16),
        ],
        compiler_params=pltpu.CompilerParams(vmem_limit_bytes=24 * 2**20),
        cost_estimate=pl.CostEstimate(
            flops=2 * slots * size**3, bytes_accessed=2 * slots * size**2, transcendentals=0
        ),
        name="other_terms",
    )(
        in_smem(place), in_smem(target), in_smem(others), in_vmem(pair), in_vmem(following), in_vmem(total),
        in_vmem(left), in_vmem(right),
    )
    received = lax.all_to_all(parts, "mpo", 0, 0)
    summed = received[0].astype(jnp.float32)
    for g in range(1, groups):
        summed += received[g].astype(jnp.float32)
    return jnp.where(keep != 0, summed, 0.0)


def solution(mesh):
    placed = (
        P("blk", None, None),
        P("blk"),
        P(("blk", "mpo"), None, None),
        P(("blk", "mpo"), None, None),
        P(("blk", "mpo")),
        P(("blk", "mpo")),
    )
    return jax.shard_map(
        body, mesh=mesh, in_specs=placed, out_specs=P("blk", "mpo", None), check_vma=False
    )
```

time: 120 us -> 39.9 us (0.33)
  waiting for transfers between devices: 63.8 us -> 1.88 us
  between operations: 14.1 us -> 0.04 us
  blocking collectives: 0 us -> 13.9 us
  matrix products: 12.4 us -> 0 us
  Pallas kernels: 0 us -> 6.1 us
  other arithmetic: 6.37 us -> 0.78 us
  local copies, waits for them, and re-layouts: 5.44 us -> 0 us
    unnamed x2 -> x0, waiting for transfers between devices: 57.8 us -> none
    all_to_all x0 -> x1, blocking collectives: none -> 13.9 us  [body(): received = lax.all_to_all(parts, 'mpo', 0, 0)]
    dot_general x2 -> x0, matrix products: 12.4 us -> none  [the longest x1 6.82 us: body(): jnp.einsum('pt,til->pil', onehot, second, precision=lax.Precision.HIGHEST)]
    pallas_call x0 -> x3, Pallas kernels: none -> 6.1 us  [the longest x1 3.66 us: body(): pl.pallas_call(own_kernel, out_shape=(pltpu.VMEM((sectors + 1, size, size...]
    ppermute x2, waiting for transfers between devices: 5.99 us -> 1.88 us  [the longest x1 1.26 us: body(): following = lax.ppermute(masked, 'blk', next_chip)]
    gather x1 -> x0, local copies, waits for them, and re-layouts: 3.4 us -> none  [body(): picked = jnp.take(window, local_index, axis=0)]
    concatenate x1 -> x0, other arithmetic: 2.37 us -> none  [extended(): block = jnp.concatenate([low, block, high], axis=dim)]
    select_n x2 -> x1, other arithmetic: 2.37 us -> 0.78 us  [body(): return jnp.where(keep != 0, summed, 0.0)]
  transfers between devices with their start and end apart: 3 -> 2, of which waited for: 3 -> 2; matrix products, arithmetic and copies ran while one was open for 2% -> 0% of each run, Pallas kernels for 0% -> 9%
where the time goes in v2:
time: 39.9 us; the launch traced here: 39.4 us
  starting transfers between devices  16.7 us (42%)
  blocking collectives  13.9 us (35%)
  Pallas kernels  6.1 us (15%)
  waiting for transfers between devices  1.88 us (5%)
  other arithmetic  0.78 us (2%)
    ppermute x1, starting transfers between devices, body(): following = lax.ppermute(masked, 'blk', next_chip)  14.8 us
    all_to_all x1, blocking collectives, body(): received = lax.all_to_all(parts, 'mpo', 0, 0)  13.9 us
    pallas_call x1, Pallas kernels, body(): pl.pallas_call(own_kernel, out_shape=(pltpu.VMEM((sectors + 1, size, size...  3.66 us
    ppermute x1, starting transfers between devices, body(): pair = lax.ppermute(copied, 'blk', same_chip)  1.92 us
    pallas_call x1, Pallas kernels, body(): pl.pallas_call(other_kernel, out_shape=pltpu.VMEM((groups, sectors, part_...  1.29 us
    ppermute x1, waiting for transfers between devices, body(): following = lax.ppermute(masked, 'blk', next_chip)  1.26 us
    pallas_call x1, Pallas kernels, body(): pl.pallas_call(mask_kernel, out_shape=pltpu.VMEM(psi.shape, psi.dtype), i...  1.15 us
  transfers between devices with their start and end apart: 2, of which 2 were waited for; matrix products, arithmetic and copies ran while one was open for 0% of the time, Pallas kernels for 9%

profile of v2, /device:TPU:56, one launch (start us, length us, event | category | flops | bytes accessed | tf_op | source)
XLA Modules:
  0.0 39.4 jit_solution(13491128205530356898)
XLA Ops:
  0.0 1.2 %masked.1.own_ref = bf16[4,256,256]{2,1,0:T(8,128)(2,1)S(1)} custom-call(s32[4]{0:T(128)} %class_hbm.3, bf16[4,256,256]{2,1,0:T(8,128)(2,1)} %psi_hbm.1), custom_call_target="tpu_custom_call" | custom-call | tf_op jit(solution)/shard_map/masked/pallas_call | solution.py:156
  1.2 14.8 %collective-permute-start.1 = (bf16[4,256,256]{2,1,0:T(8,128)(2,1)S(1)}, bf16[4,256,256]{2,1,0:T(8,128)(2,1)S(1)}, u32[]{:S(2)}, u32[]{:S(2)}) collective-permute-start(bf16[4,256,256]{2,1,0:T(8,128)(2,1)S(1)} %masked.1.own_ref), channel_id=1, source_target_pairs={{4,8},{8,4},{12,16},{16,12},{20,24},{24,20},{28,32},{32,28},{36,40... | collective-permute-start | bytes 1572872 | tf_op jit(solution)/shard_map/ppermute | solution.py:169
  16.0 3.7 %own_terms.1 = (f32[5,256,256]{2,1,0:T(8,128)S(1)}, bf16[16,256,256]{2,1,0:T(8,128)(2,1)S(1)}, bf16[16,256,256]{2,1,0:T(8,128)(2,1)S(1)}, f32[4,64,256]{2,1,0:T(...) custom-call(s32[4]{0:T(128)} %class_hbm.3, s32[16]{0:T(128)} %source_hbm.1, ...), custom_call_target="tpu_custom_call" | custom-call | flops 805306368 | bytes 4194304 | tf_op jit(solution)/shard_map/own_terms/pallas_call | solution.py:170
  19.6 1.9 %collective-permute-start = (bf16[4,256,256]{2,1,0:T(8,128)(2,1)S(1)}, bf16[4,256,256]{2,1,0:T(8,128)(2,1)S(1)}, u32[]{:S(2)}, u32[]{:S(2)}) collective-permute-start(bf16[4,256,256]{2,1,0:T(8,128)(2,1)S(1)} %get-tuple-element.17), channel_id=1, source_target_pairs={{0,4},{4,0},{8,12},{12,8},{16,20},{20,16},{24,28},{28,24},{32,36},... | collective-permute-start | bytes 1572872 | tf_op jit(solution)/shard_map/ppermute | solution.py:197
  21.6 1.3 %collective-permute-done.1.next_ref = bf16[4,256,256]{2,1,0:T(8,128)(2,1)S(1)} collective-permute-done((bf16[4,256,256]{2,1,0:T(8,128)(2,1)S(1)}, bf16[4,256,256]{2,1,0:T(8,128)(2,1)S(1)}, u32[]{:S(2)}, u32[]{:S(2)}) %collective-permute-start.1) | collective-permute-done | bytes 524320 | tf_op jit(solution)/shard_map/ppermute | solution.py:169
  22.8 0.6 %collective-permute-done.pair_ref = bf16[4,256,256]{2,1,0:T(8,128)(2,1)S(1)} collective-permute-done((bf16[4,256,256]{2,1,0:T(8,128)(2,1)S(1)}, bf16[4,256,256]{2,1,0:T(8,128)(2,1)S(1)}, u32[]{:S(2)}, u32[]{:S(2)}) %collective-permute-start) | collective-permute-done | bytes 524320 | tf_op jit(solution)/shard_map/ppermute | solution.py:197
  23.4 1.3 %other_terms.1 = bf16[4,4,64,256]{3,2,1,0:T(8,128)(2,1)S(1)} custom-call(s32[16]{0:T(128)S(4)} %get-tuple-element.14.place_ref, s32[16]{0:T(128)S(4)} %get-tuple-element.15.target_ref, s32[17]{0:T(128)S(4)} %get-tuple-element.16.others, bf16[4,256,256]{2,1,0:T(8,128)(2,1)S(1)} %collective-permute-done.pair_ref, ...), custom_call_target="tpu_custom_call" | custom-call | flops 536870912 | bytes 2097152 | tf_op jit(solution)/shard_map/other_terms/pallas_call | solution.py:198
  24.7 13.9 %all_to_all.5 = bf16[4,4,64,256]{3,2,1,0:T(8,128)(2,1)S(1)} all-to-all(bf16[4,4,64,256]{3,2,1,0:T(8,128)(2,1)S(1)} %other_terms.1), channel_id=1, replica_groups=mesh['blk'=192,'mpo'=4] {'mpo'}, dimensions={0} | all-to-all | bytes 1048576 | tf_op jit(solution)/shard_map/all_to_all | solution.py:216
  38.6 0.8 %bitcast_select_fusion = f32[4,64,256]{2,1,0:T(8,128)} fusion(f32[4,64,256]{2,1,0:T(8,128)S(1)} %get-tuple-element.13, bf16[4,4,64,256]{3,2,1,0:T(8,128)(2,1)S(1)} %all_to_all.5), kind=kLoop, calls=%fused_computation | loop fusion | flops 589824 | bytes 1048576 | tf_op jit(solution)/shard_map/jit(_where)/select_n | solution.py:220
Async XLA Ops:
  1.2 21.7 %collective-permute-start.1 = (bf16[4,256,256]{2,1,0:T(8,128)(2,1)S(1)}, bf16[4,256,256]{2,1,0:T(8,128)(2,1)S(1)}, u32[]{:S(2)}, u32[]{:S(2)}) collective-permute-start(bf16[4,256,256]{2,1,0:T(8,128)(2,1)S(1)} %masked.1.own_ref), channel_id=1, source_target_pairs={{4,8},{8,4},{12,16},{16,12},{20,24},{24,20},{28,32},{32,28},{36,40... | collective-permute-start | bytes 1572872 | tf_op jit(solution)/shard_map/ppermute | solution.py:169
  19.6 3.8 %collective-permute-start = (bf16[4,256,256]{2,1,0:T(8,128)(2,1)S(1)}, bf16[4,256,256]{2,1,0:T(8,128)(2,1)S(1)}, u32[]{:S(2)}, u32[]{:S(2)}) collective-permute-start(bf16[4,256,256]{2,1,0:T(8,128)(2,1)S(1)} %get-tuple-element.17), channel_id=1, source_target_pairs={{0,4},{4,0},{8,12},{12,8},{16,20},{20,16},{24,28},{28,24},{32,36},... | collective-permute-start | bytes 1572872 | tf_op jit(solution)/shard_map/ppermute | solution.py:197

commit v3 on v0

v3 whole, which is shorter than its diff:
```python
import jax
import jax.numpy as jnp
from jax import lax
from jax.experimental import pallas as pl
from jax.experimental.pallas import tpu as pltpu
from jax.sharding import PartitionSpec as P

SMEM = pl.BlockSpec(memory_space=pltpu.SMEM)
VMEM = pl.BlockSpec(memory_space=pltpu.VMEM)
ANY = pl.BlockSpec(memory_space=pl.ANY)
DMA = pltpu.SemaphoreType.DMA
TOGETHER = 4


def in_vmem(x):
    return pltpu.with_memory_space_constraint(x, pltpu.VMEM)


def in_hbm(x):
    return pltpu.with_memory_space_constraint(x, pltpu.HBM)


def in_smem(x):
    return pltpu.with_memory_space_constraint(x, pltpu.SMEM)


def mask_rows(block, sector_class):
    size = block.shape[0]
    quarter = size // 4
    cols = lax.broadcasted_iota(jnp.int32, (quarter, size), 1)
    pieces = []
    for q in range(4):
        live = jnp.where(q < sector_class, sector_class * quarter, 0)
        piece = block[q * quarter : (q + 1) * quarter]
        pieces.append(jnp.where(cols < live, piece, jnp.zeros_like(piece)))
    return jnp.concatenate(pieces, axis=0)


def fill_queue(queue, chosen, source_ref, target_ref):
    slots = source_ref.shape[0]
    for t in range(slots):
        queue[t] = 0
    count = jnp.int32(0)
    for t in range(slots):
        take = jnp.logical_and(target_ref[t] >= 0, chosen(source_ref[t]))
        queue[count] = jnp.where(take, t, 0)
        count += take.astype(jnp.int32)
    queue[slots] = count


def add_together(n_first, together, queue, block_of, target_ref, left_ref, right_ref, total):
    sectors = total.shape[0] - 1
    count = queue[queue.shape[0] - 1]
    places = [n_first + j for j in range(together)]
    picked = [queue[n] for n in places]
    products = [
        jnp.dot(left_ref[t], block_of(t), preferred_element_type=jnp.float32).astype(jnp.bfloat16)
        for t in picked
    ]
    terms = [
        lax.dot_general(
            product, right_ref[t], (((1,), (1,)), ((), ())), preferred_element_type=jnp.float32
        )
        for product, t in zip(products, picked)
    ]
    for n, t, term in zip(places, picked, terms):
        total[jnp.where(n < count, target_ref[t], sectors)] += term


def add_terms(queue, block_of, target_ref, left_ref, right_ref, total, first=0):
    refs = (queue, block_of, target_ref, left_ref, right_ref, total)
    count = queue[queue.shape[0] - 1]
    if first:
        add_together(0, first, *refs)

    def step(i, carry):
        add_together(first + i * TOGETHER, TOGETHER, *refs)
        return carry

    rest = jnp.maximum(count - first, 0)
    lax.fori_loop(0, (rest + TOGETHER - 1) // TOGETHER, step, 0)


def load_terms(
    hbm, own_ref, total, left_ref, right_ref, target_ref, place_ref, others,
    source_ref, queue, small_sems, left_sems, right_sems,
):
    source_hbm, target_hbm, left_hbm, right_hbm = hbm
    slots, size, _ = left_ref.shape
    sectors = own_ref.shape[0]
    first = lax.axis_index("blk") * sectors
    chip_first = lax.axis_index("blk") // 2 * 2 * sectors
    small = [
        pltpu.make_async_copy(a, b, small_sems.at[i])
        for i, (a, b) in enumerate(((source_hbm, source_ref), (target_hbm, target_ref)))
    ]
    large = []
    for t in range(slots):
        large.append(pltpu.make_async_copy(left_hbm.at[t], left_ref.at[t], left_sems.at[t]))
        large.append(pltpu.make_async_copy(right_hbm.at[t], right_ref.at[t], right_sems.at[t]))
    for copy in small + large:
        copy.start()
    total[...] = jnp.zeros_like(total)
    for copy in small:
        copy.wait()
    def is_own(source):
        return jnp.logical_and(source >= first, source < first + sectors)

    fill_queue(queue, is_own, source_ref, target_ref)
    fill_queue(others, lambda source: jnp.logical_not(is_own(source)), source_ref, target_ref)
    for t in range(slots):
        near = jnp.logical_and(
            source_ref[t] >= chip_first, source_ref[t] < chip_first + 2 * sectors
        )
        place_ref[t] = lax.rem(source_ref[t], sectors) + jnp.where(near, 0, sectors)
    for copy in large:
        copy.wait()
    add_terms(
        queue,
        lambda t: own_ref[lax.rem(place_ref[t], sectors)],
        target_ref, left_ref, right_ref, total,
    )


def early_kernel(
    class_hbm, psi_hbm, source_hbm, target_hbm, left_hbm, right_hbm,
    masked_ref, class_ref, total, left_ref, right_ref, target_ref, place_ref, others,
    psi_ref, source_ref, queue, class_sem, psi_sems, small_sems, left_sems, right_sems,
):
    sectors = psi_ref.shape[0]
    load_class = pltpu.make_async_copy(class_hbm, class_ref, class_sem)
    blocks = [
        pltpu.make_async_copy(psi_hbm.at[s], psi_ref.at[s], psi_sems.at[s]) for s in range(sectors)
    ]
    load_class.start()
    for copy in blocks:
        copy.start()
    load_class.wait()
    for s in range(sectors):
        blocks[s].wait()
        masked_ref[s] = mask_rows(psi_ref[s], class_ref[s])

    @pl.when(lax.rem(lax.axis_index("blk"), 2) == 0)
    def _():
        load_terms(
            (source_hbm, target_hbm, left_hbm, right_hbm),
            masked_ref, total, left_ref, right_ref, target_ref, place_ref, others,
            source_ref, queue, small_sems, left_sems, right_sems,
        )


def late_kernel(
    source_hbm, target_hbm, left_hbm, right_hbm, own_ref, classes,
    copy_ref, keep_ref, total, left_ref, right_ref, target_ref, place_ref, others,
    source_ref, queue, small_sems, left_sems, right_sems,
):
    sectors, part_rows, size = keep_ref.shape
    copy_ref[...] = own_ref[...]
    first_row = lax.axis_index("mpo") * part_rows
    rows = first_row + lax.broadcasted_iota(jnp.int32, (part_rows, size), 0)
    cols = lax.broadcasted_iota(jnp.int32, (part_rows, size), 1)
    for s in range(sectors):
        live = classes[s] * (size // 4)
        keep_ref[s] = ((rows < live) & (cols < live)).astype(jnp.float32)

    @pl.when(lax.rem(lax.axis_index("blk"), 2) == 1)
    def _():
        load_terms(
            (source_hbm, target_hbm, left_hbm, right_hbm),
            own_ref, total, left_ref, right_ref, target_ref, place_ref, others,
            source_ref, queue, small_sems, left_sems, right_sems,
        )


def other_kernel(
    even_target, even_place, even_others, odd_target, odd_place, odd_others, pair_ref, next_ref,
    even_given, odd_given, even_left, even_right, odd_left, odd_right,
    parts_ref, even_total, odd_total,
):
    groups, sectors, part_rows, _ = parts_ref.shape
    odd = lax.rem(lax.axis_index("blk"), 2)

    def finish(place_ref, target_ref, others, left_ref, right_ref, total):
        def block_of(t):
            at = lax.rem(place_ref[t], sectors)
            return jnp.where(place_ref[t] < sectors, pair_ref[at], next_ref[at])

        add_terms(others, block_of, target_ref, left_ref, right_ref, total, 8)
        for g in range(groups):
            for s in range(sectors):
                parts_ref[g, s] = total[s, g * part_rows : (g + 1) * part_rows, :].astype(
                    parts_ref.dtype
                )

    @pl.when(odd == 0)
    def _():
        finish(even_place, even_target, even_others, even_left, even_right, even_total)

    @pl.when(odd == 1)
    def _():
        finish(odd_place, odd_target, odd_others, odd_left, odd_right, odd_total)


def body(psi, sector_class, left_env, right_env, term_source, term_target):
    sectors, size, _ = psi.shape
    slots = left_env.shape[0]
    owners = lax.axis_size("blk")
    groups = lax.axis_size("mpo")
    part_rows = size // groups
    same_chip = [(i, i ^ 1) for i in range(owners)]
    next_chip = [(i, i - 1 if i % 2 == 0 else i + 1) for i in range(1, owners - 1)]
    params = pltpu.CompilerParams(vmem_limit_bytes=24 * 2**20)
    sums = pltpu.VMEM((sectors + 1, size, size), jnp.float32)
    numbers = pltpu.SMEM((slots,), jnp.int32)
    queue = pltpu.SMEM((slots + 1,), jnp.int32)
    sector_blocks = pltpu.VMEM(psi.shape, psi.dtype)
    loaded = (
        sums,
        pltpu.VMEM(left_env.shape, left_env.dtype),
        pltpu.VMEM(right_env.shape, right_env.dtype),
        numbers, numbers, queue,
    )
    loaded_specs = (VMEM,) * 3 + (SMEM,) * 3
    load_scratch = [numbers, queue]
    load_sems = [DMA((2,)), DMA((slots,)), DMA((slots,))]
    tables = tuple(in_hbm(x) for x in (term_source, term_target, left_env, right_env))

    def cost(share):
        return pl.CostEstimate(
            flops=int(4 * slots * size**3 * share),
            bytes_accessed=int(4 * slots * size**2 * share),
            transcendentals=0,
        )

    masked, classes, *even = pl.pallas_call(
        early_kernel,
        out_shape=(sector_blocks, pltpu.SMEM((sectors,), jnp.int32), *loaded),
        in_specs=[ANY] * 6,
        out_specs=(VMEM, SMEM, *loaded_specs),
        scratch_shapes=[sector_blocks, *load_scratch, DMA, DMA((sectors,)), *load_sems],
        compiler_params=params,
        name="early_terms",
    )(in_hbm(sector_class), in_hbm(psi), *tables)
    following = lax.ppermute(masked, "blk", next_chip)
    copied, keep, *odd = pl.pallas_call(
        late_kernel,
        out_shape=(sector_blocks, pltpu.VMEM((sectors, part_rows, size), jnp.float32), *loaded),
        in_specs=[ANY] * 4 + [VMEM, SMEM],
        out_specs=(VMEM, VMEM, *loaded_specs),
        scratch_shapes=[*load_scratch, *load_sems],
        compiler_params=params,
        cost_estimate=cost(1),
        name="late_terms",
    )(*tables, in_vmem(masked), in_smem(classes))
    pair = lax.ppermute(copied, "blk", same_chip)
    even_total, even_left, even_right, *even_lists = even
    odd_total, odd_left, odd_right, *odd_lists = odd
    parts, _, _ = pl.pallas_call(
        other_kernel,
        out_shape=(
            pltpu.VMEM((groups, sectors, part_rows, size), jnp.bfloat16), sums, sums,
        ),
        in_specs=[SMEM] * 6 + [VMEM] * 8,
        out_specs=(VMEM,) * 3,
        input_output_aliases={8: 1, 9: 2},
        compiler_params=params,
        cost_estimate=cost(0.5),
        name="other_terms",
    )(
        *(in_smem(x) for x in (*even_lists, *odd_lists)),
        *(in_vmem(x) for x in (pair, following, even_total, odd_total)),
        *(in_vmem(x) for x in (even_left, even_right, odd_left, odd_right)),
    )
    received = lax.all_to_all(parts, "mpo", 0, 0)
    summed = received[0].astype(jnp.float32)
    for g in range(1, groups):
        summed += received[g].astype(jnp.float32)
    return jnp.where(keep != 0, summed, 0.0)


def solution(mesh):
    placed = (
        P("blk", None, None),
        P("blk"),
        P(("blk", "mpo"), None, None),
        P(("blk", "mpo"), None, None),
        P(("blk", "mpo")),
        P(("blk", "mpo")),
    )
    return jax.shard_map(
        body, mesh=mesh, in_specs=placed, out_specs=P("blk", "mpo", None), check_vma=False
    )
```

time: 120 us -> 37.6 us (0.31)
  waiting for transfers between devices: 63.8 us -> 4.55 us
  between operations: 14.1 us -> 0.04 us
  blocking collectives: 0 us -> 12.7 us
  matrix products: 12.4 us -> 0 us
  Pallas kernels: 0 us -> 5.81 us
  other arithmetic: 6.37 us -> 0.78 us
  local copies, waits for them, and re-layouts: 5.44 us -> 0 us
  starting transfers between devices: 16.7 us -> 13.6 us
    unnamed x2 -> x0, waiting for transfers between devices: 57.8 us -> none
    all_to_all x0 -> x1, blocking collectives: none -> 12.7 us  [body(): received = lax.all_to_all(parts, 'mpo', 0, 0)]
    dot_general x2 -> x0, matrix products: 12.4 us -> none  [the longest x1 6.82 us: body(): jnp.einsum('pt,til->pil', onehot, second, precision=lax.Precision.HIGHEST)]
    pallas_call x0 -> x3, Pallas kernels: none -> 5.81 us  [the longest x1 4.62 us: body(): pl.pallas_call(early_kernel, out_shape=(sector_blocks, pltpu.SMEM((sector...]
    gather x1 -> x0, local copies, waits for them, and re-layouts: 3.4 us -> none  [body(): picked = jnp.take(window, local_index, axis=0)]
    ppermute x2, starting transfers between devices: 16.7 us -> 13.6 us  [the longest x1 11.7 us: body(): following = lax.ppermute(masked, 'blk', next_chip)]
    concatenate x1 -> x0, other arithmetic: 2.37 us -> none  [extended(): block = jnp.concatenate([low, block, high], axis=dim)]
    select_n x2 -> x1, other arithmetic: 2.37 us -> 0.78 us  [body(): return jnp.where(keep != 0, summed, 0.0)]
  transfers between devices with their start and end apart: 3 -> 2, of which waited for: 3 -> 1; matrix products, arithmetic and copies ran while one was open for 2% -> 0% of each run, Pallas kernels for 0% -> 1%
where the time goes in v3:
time: 37.6 us; the launch traced here: 37.4 us
  starting transfers between devices  13.6 us (36%)
  blocking collectives  12.7 us (34%)
  Pallas kernels  5.81 us (15%)
  waiting for transfers between devices  4.55 us (12%)
  other arithmetic  0.78 us (2%)
    all_to_all x1, blocking collectives, body(): received = lax.all_to_all(parts, 'mpo', 0, 0)  12.7 us
    ppermute x1, starting transfers between devices, body(): following = lax.ppermute(masked, 'blk', next_chip)  11.7 us
    pallas_call x1, Pallas kernels, body(): pl.pallas_call(early_kernel, out_shape=(sector_blocks, pltpu.SMEM((sector...  4.62 us
    ppermute x1, waiting for transfers between devices, body(): following = lax.ppermute(masked, 'blk', next_chip)  4.55 us
    ppermute x1, starting transfers between devices, body(): pair = lax.ppermute(copied, 'blk', same_chip)  1.92 us
    pallas_call x1, Pallas kernels, body(): pl.pallas_call(other_kernel, out_shape=(pltpu.VMEM((groups, sectors, part...  0.83 us
    select_n x1, other arithmetic, body(): return jnp.where(keep != 0, summed, 0.0)  0.78 us
  transfers between devices with their start and end apart: 2, of which 1 were waited for; matrix products, arithmetic and copies ran while one was open for 0% of the time, Pallas kernels for 1%

profile of v3, /device:TPU:56, one launch (start us, length us, event | category | flops | bytes accessed | tf_op | source)
XLA Modules:
  0.0 37.4 jit_solution(11011338530938586501)
XLA Ops:
  0.0 4.6 %early_terms.1 = (bf16[4,256,256]{2,1,0:T(8,128)(2,1)S(1)}, s32[4]{0:T(128)S(4)}, f32[5,256,256]{2,1,0:T(8,128)S(1)}, bf16[16,256,256]{2,1,0:T(8,128)(2,1)S(1)},...) custom-call(s32[4]{0:T(128)} %class_hbm.1, bf16[4,256,256]{2,1,0:T(8,128)(2,1)} %psi_hbm.1, ...), custom_call_target="tpu_custom_call" | custom-call | tf_op jit(solution)/shard_map/early_terms/pallas_call | solution.py:235
  4.6 11.7 %collective-permute-start.1 = (bf16[4,256,256]{2,1,0:T(8,128)(2,1)S(1)}, bf16[4,256,256]{2,1,0:T(8,128)(2,1)S(1)}, u32[]{:S(2)}, u32[]{:S(2)}) collective-permute-start(bf16[4,256,256]{2,1,0:T(8,128)(2,1)S(1)} %get-tuple-element.22.own_ref), channel_id=1, source_target_pairs={{4,8},{8,4},{12,16},{16,12},{20,24},{24,20},{28,32},{32,28},{36,40... | collective-permute-start | bytes 1572872 | tf_op jit(solution)/shard_map/ppermute | solution.py:244
  16.3 0.4 late_terms.1
  16.7 1.9 %collective-permute-start = (bf16[4,256,256]{2,1,0:T(8,128)(2,1)S(1)}, bf16[4,256,256]{2,1,0:T(8,128)(2,1)S(1)}, u32[]{:S(2)}, u32[]{:S(2)}) collective-permute-start(bf16[4,256,256]{2,1,0:T(8,128)(2,1)S(1)} %get-tuple-element.31), channel_id=1, source_target_pairs={{0,4},{4,0},{8,12},{12,8},{16,20},{20,16},{24,28},{28,24},{32,36},... | collective-permute-start | bytes 1572872 | tf_op jit(solution)/shard_map/ppermute | solution.py:255
  18.6 4.6 %collective-permute-done.1.next_ref = bf16[4,256,256]{2,1,0:T(8,128)(2,1)S(1)} collective-permute-done((bf16[4,256,256]{2,1,0:T(8,128)(2,1)S(1)}, bf16[4,256,256]{2,1,0:T(8,128)(2,1)S(1)}, u32[]{:S(2)}, u32[]{:S(2)}) %collective-permute-start.1) | collective-permute-done | bytes 524320 | tf_op jit(solution)/shard_map/ppermute | solution.py:244
  23.1 0.0 collective-permute-done.pair_ref
  23.1 0.8 %other_terms.1 = (bf16[4,4,64,256]{3,2,1,0:T(8,128)(2,1)S(1)}, f32[5,256,256]{2,1,0:T(8,128)S(1)}, f32[5,256,256]{2,1,0:T(8,128)S(1)}) custom-call(s32[16]{0:T(128)S(4)} %get-tuple-element.25.even_target, s32[16]{0:T(128)S(4)} %get-tuple-element.26.even_place, s32[17]{0:T(128)S(4)} %get-tuple-element.27.even_others, ...), custom_call_target="tpu_custom_call", output_to_operand_aliasing={{1}: (8, {}), {2}: (9, {})} | custom-call | flops 536870912 | bytes 2097152 | tf_op jit(solution)/shard_map/other_terms/pallas_call | solution.py:258
  24.0 12.7 %all_to_all.5 = bf16[4,4,64,256]{3,2,1,0:T(8,128)(2,1)S(1)} all-to-all(bf16[4,4,64,256]{3,2,1,0:T(8,128)(2,1)S(1)} %get-tuple-element.38), channel_id=1, replica_groups=mesh['blk'=192,'mpo'=4] {'mpo'}, dimensions={0} | all-to-all | bytes 1048576 | tf_op jit(solution)/shard_map/all_to_all | solution.py:274
  36.6 0.8 %bitcast_select_fusion = f32[4,64,256]{2,1,0:T(8,128)} fusion(f32[4,64,256]{2,1,0:T(8,128)S(1)} %get-tuple-element.24, bf16[4,4,64,256]{3,2,1,0:T(8,128)(2,1)S(1)} %all_to_all.5), kind=kLoop, calls=%fused_computation | loop fusion | flops 589824 | bytes 1048576 | tf_op jit(solution)/shard_map/jit(_where)/select_n | solution.py:278
Async XLA Ops:
  4.6 18.5 %collective-permute-start.1 = (bf16[4,256,256]{2,1,0:T(8,128)(2,1)S(1)}, bf16[4,256,256]{2,1,0:T(8,128)(2,1)S(1)}, u32[]{:S(2)}, u32[]{:S(2)}) collective-permute-start(bf16[4,256,256]{2,1,0:T(8,128)(2,1)S(1)} %get-tuple-element.22.own_ref), channel_id=1, source_target_pairs={{4,8},{8,4},{12,16},{16,12},{20,24},{24,20},{28,32},{32,28},{36,40... | collective-permute-start | bytes 1572872 | tf_op jit(solution)/shard_map/ppermute | solution.py:244
  16.7 6.5 %collective-permute-start = (bf16[4,256,256]{2,1,0:T(8,128)(2,1)S(1)}, bf16[4,256,256]{2,1,0:T(8,128)(2,1)S(1)}, u32[]{:S(2)}, u32[]{:S(2)}) collective-permute-start(bf16[4,256,256]{2,1,0:T(8,128)(2,1)S(1)} %get-tuple-element.31), channel_id=1, source_target_pairs={{0,4},{4,0},{8,12},{12,8},{16,20},{20,16},{24,28},{28,24},{32,36},... | collective-permute-start | bytes 1572872 | tf_op jit(solution)/shard_map/ppermute | solution.py:255

commit v4 on v3

v4 whole, which is shorter than its diff:
```python
import jax
import jax.numpy as jnp
from jax import lax
from jax.experimental import pallas as pl
from jax.experimental.pallas import tpu as pltpu
from jax.sharding import PartitionSpec as P

SMEM = pl.BlockSpec(memory_space=pltpu.SMEM)
VMEM = pl.BlockSpec(memory_space=pltpu.VMEM)
ANY = pl.BlockSpec(memory_space=pl.ANY)
DMA = pltpu.SemaphoreType.DMA
TOGETHER = 4
TILE_ROWS = 16


def in_vmem(x):
    return pltpu.with_memory_space_constraint(x, pltpu.VMEM)


def in_hbm(x):
    return pltpu.with_memory_space_constraint(x, pltpu.HBM)


def in_smem(x):
    return pltpu.with_memory_space_constraint(x, pltpu.SMEM)


def mask_rows(block, sector_class):
    size = block.shape[0]
    quarter = size // 4
    cols = lax.broadcasted_iota(jnp.int32, (TILE_ROWS, size), 1)
    keep = (cols < sector_class * quarter).astype(block.dtype)
    pieces = []
    for q in range(4):
        rows = keep * jnp.where(q < sector_class, 1.0, 0.0).astype(block.dtype)
        for r in range(0, quarter, TILE_ROWS):
            first = q * quarter + r
            pieces.append(block[first : first + TILE_ROWS] * rows)
    return jnp.concatenate(pieces, axis=0)


def fill_queue(queue, chosen, source_ref, target_ref):
    slots = source_ref.shape[0]
    for t in range(slots):
        queue[t] = 0
    count = jnp.int32(0)
    for t in range(slots):
        take = jnp.logical_and(target_ref[t] >= 0, chosen(source_ref[t]))
        queue[count] = jnp.where(take, t, 0)
        count += take.astype(jnp.int32)
    queue[slots] = count


def add_together(n_first, together, queue, block_of, target_ref, left_ref, right_ref, total):
    sectors = total.shape[0] - 1
    count = queue[queue.shape[0] - 1]
    places = [n_first + j for j in range(together)]
    picked = [queue[n] for n in places]
    products = [
        jnp.dot(left_ref[t], block_of(t), preferred_element_type=jnp.float32).astype(jnp.bfloat16)
        for t in picked
    ]
    terms = [
        lax.dot_general(
            product, right_ref[t], (((1,), (1,)), ((), ())), preferred_element_type=jnp.float32
        )
        for product, t in zip(products, picked)
    ]
    for n, t, term in zip(places, picked, terms):
        total[jnp.where(n < count, target_ref[t], sectors)] += term


def add_terms(queue, block_of, target_ref, left_ref, right_ref, total, first=0):
    refs = (queue, block_of, target_ref, left_ref, right_ref, total)
    count = queue[queue.shape[0] - 1]
    if first:
        add_together(0, first, *refs)

    def step(i, carry):
        add_together(first + i * TOGETHER, TOGETHER, *refs)
        return carry

    rest = jnp.maximum(count - first, 0)
    lax.fori_loop(0, (rest + TOGETHER - 1) // TOGETHER, step, 0)


def load_terms(
    hbm, own_ref, total, left_ref, right_ref, target_ref, place_ref, pair_queue, next_queue,
    source_ref, queue, small_sems, env_sems,
):
    source_hbm, target_hbm, left_hbm, right_hbm = hbm
    slots, size, _ = left_ref.shape
    sectors = total.shape[0] - 1
    first = lax.axis_index("blk") * sectors
    chip_first = lax.axis_index("blk") // 2 * 2 * sectors
    small = [
        pltpu.make_async_copy(a, b, small_sems.at[i])
        for i, (a, b) in enumerate(((source_hbm, source_ref), (target_hbm, target_ref)))
    ]
    piece = slots // 4
    whole = []
    for copy in small:
        copy.start()
    for i, (a, b) in enumerate(((left_hbm, left_ref), (right_hbm, right_ref))):
        for t in range(0, slots, piece):
            part = pl.ds(t, piece)
            pltpu.make_async_copy(a.at[part], b.at[part], env_sems.at[i]).start()
        whole.append(pltpu.make_async_copy(a, b, env_sems.at[i]))
    total[...] = jnp.zeros_like(total)
    for copy in small:
        copy.wait()
    def is_own(source):
        return jnp.logical_and(source >= first, source < first + sectors)

    fill_queue(queue, is_own, source_ref, target_ref)
    def is_near(source):
        return jnp.logical_and(source >= chip_first, source < chip_first + 2 * sectors)

    fill_queue(
        pair_queue,
        lambda source: jnp.logical_and(is_near(source), jnp.logical_not(is_own(source))),
        source_ref,
        target_ref,
    )
    fill_queue(next_queue, lambda source: jnp.logical_not(is_near(source)), source_ref, target_ref)
    for t in range(slots):
        place_ref[t] = lax.rem(source_ref[t], sectors)
    for copy in whole:
        copy.wait()
    add_terms(
        queue,
        lambda t: own_ref[pl.ds(pl.multiple_of(place_ref[t] * size, size), size), :],
        target_ref, left_ref, right_ref, total,
    )


def mask_kernel(class_hbm, psi_hbm, masked_ref, class_ref, psi_ref, class_sem, psi_sem):
    sectors, size, _ = psi_ref.shape
    load_class = pltpu.make_async_copy(class_hbm, class_ref, class_sem)
    load_psi = pltpu.make_async_copy(psi_hbm, psi_ref, psi_sem)
    load_class.start()
    load_psi.start()
    masked_ref[sectors * size :] = jnp.zeros((TILE_ROWS, size), masked_ref.dtype)
    load_class.wait()
    load_psi.wait()
    for s in range(sectors):
        masked_ref[s * size : (s + 1) * size] = mask_rows(psi_ref[s], class_ref[s])


def early_kernel(
    source_hbm, target_hbm, left_hbm, right_hbm, given_ref,
    masked_ref, total, left_ref, right_ref, target_ref, place_ref, pair_queue, next_queue,
    source_ref, queue, small_sems, env_sems,
):
    @pl.when(lax.rem(lax.axis_index("blk"), 2) == 0)
    def _():
        load_terms(
            (source_hbm, target_hbm, left_hbm, right_hbm),
            masked_ref, total, left_ref, right_ref, target_ref, place_ref, pair_queue, next_queue,
            source_ref, queue, small_sems, env_sems,
        )


def late_kernel(
    source_hbm, target_hbm, left_hbm, right_hbm, own_ref, classes,
    copy_ref, keep_ref, total, left_ref, right_ref, target_ref, place_ref, pair_queue, next_queue,
    source_ref, queue, small_sems, env_sems,
):
    sectors, part_rows, size = keep_ref.shape
    for s in range(sectors):
        copy_ref[s] = own_ref[s * size : (s + 1) * size]
    first_row = lax.axis_index("mpo") * part_rows
    rows = first_row + lax.broadcasted_iota(jnp.int32, (part_rows, size), 0)
    cols = lax.broadcasted_iota(jnp.int32, (part_rows, size), 1)
    for s in range(sectors):
        live = classes[s] * (size // 4)
        keep_ref[s] = ((rows < live) & (cols < live)).astype(jnp.float32)

    @pl.when(lax.rem(lax.axis_index("blk"), 2) == 1)
    def _():
        load_terms(
            (source_hbm, target_hbm, left_hbm, right_hbm),
            own_ref, total, left_ref, right_ref, target_ref, place_ref, pair_queue, next_queue,
            source_ref, queue, small_sems, env_sems,
        )


def pair_kernel(
    even_target, even_place, even_queue, odd_target, odd_place, odd_queue, pair_ref,
    even_given, odd_given, even_left, even_right, odd_left, odd_right, even_total, odd_total,
):
    odd = lax.rem(lax.axis_index("blk"), 2)

    def add(place_ref, target_ref, queue, left_ref, right_ref, total):
        add_terms(queue, lambda t: pair_ref[place_ref[t]], target_ref, left_ref, right_ref, total)

    @pl.when(odd == 0)
    def _():
        add(even_place, even_target, even_queue, even_left, even_right, even_total)

    @pl.when(odd == 1)
    def _():
        add(odd_place, odd_target, odd_queue, odd_left, odd_right, odd_total)


def next_kernel(
    even_target, even_place, even_queue, odd_target, odd_place, odd_queue, next_ref,
    even_given, odd_given, even_left, even_right, odd_left, odd_right,
    parts_ref, even_total, odd_total,
):
    groups, sectors, part_rows, size = parts_ref.shape
    odd = lax.rem(lax.axis_index("blk"), 2)

    def finish(place_ref, target_ref, queue, left_ref, right_ref, total):
        def block_of(t):
            return next_ref[pl.ds(pl.multiple_of(place_ref[t] * size, size), size), :]

        add_terms(queue, block_of, target_ref, left_ref, right_ref, total, 8)
        for g in range(groups):
            for s in range(sectors):
                parts_ref[g, s] = total[s, g * part_rows : (g + 1) * part_rows, :].astype(
                    parts_ref.dtype
                )

    @pl.when(odd == 0)
    def _():
        finish(even_place, even_target, even_queue, even_left, even_right, even_total)

    @pl.when(odd == 1)
    def _():
        finish(odd_place, odd_target, odd_queue, odd_left, odd_right, odd_total)


def body(psi, sector_class, left_env, right_env, term_source, term_target):
    sectors, size, _ = psi.shape
    slots = left_env.shape[0]
    owners = lax.axis_size("blk")
    groups = lax.axis_size("mpo")
    part_rows = size // groups
    same_chip = [(i, i ^ 1) for i in range(owners)]
    next_chip = [(i, i - 1 if i % 2 == 0 else i + 1) for i in range(1, owners - 1)]
    params = pltpu.CompilerParams(vmem_limit_bytes=24 * 2**20)
    sums = pltpu.VMEM((sectors + 1, size, size), jnp.float32)
    numbers = pltpu.SMEM((slots,), jnp.int32)
    queue = pltpu.SMEM((slots + 1,), jnp.int32)
    sector_blocks = pltpu.VMEM(psi.shape, psi.dtype)
    sent_rows = pltpu.VMEM((sectors * size + TILE_ROWS, size), psi.dtype)
    loaded = (
        sums,
        pltpu.VMEM(left_env.shape, left_env.dtype),
        pltpu.VMEM(right_env.shape, right_env.dtype),
        numbers, numbers, queue, queue,
    )
    loaded_specs = (VMEM,) * 3 + (SMEM,) * 4
    load_scratch = [numbers, queue]
    load_sems = [DMA((2,)), DMA((2,))]
    tables = tuple(in_hbm(x) for x in (term_source, term_target, left_env, right_env))

    def cost(share):
        return pl.CostEstimate(
            flops=int(4 * slots * size**3 * share),
            bytes_accessed=int(4 * slots * size**2 * share),
            transcendentals=0,
        )

    masked, classes = pl.pallas_call(
        mask_kernel,
        out_shape=(sent_rows, pltpu.SMEM((sectors,), jnp.int32)),
        in_specs=[ANY] * 2,
        out_specs=(VMEM, SMEM),
        scratch_shapes=[sector_blocks, DMA, DMA],
        compiler_params=params,
        name="masked",
    )(in_hbm(sector_class), in_hbm(psi))
    masked, *even = pl.pallas_call(
        early_kernel,
        out_shape=(sent_rows, *loaded),
        in_specs=[ANY] * 4 + [VMEM],
        out_specs=(VMEM, *loaded_specs),
        input_output_aliases={4: 0},
        scratch_shapes=[*load_scratch, *load_sems],
        compiler_params=params,
        name="early_terms",
    )(*tables, in_vmem(masked))
    following = lax.ppermute(masked, "blk", next_chip)
    copied, keep, *odd = pl.pallas_call(
        late_kernel,
        out_shape=(sector_blocks, pltpu.VMEM((sectors, part_rows, size), jnp.float32), *loaded),
        in_specs=[ANY] * 4 + [VMEM, SMEM],
        out_specs=(VMEM, VMEM, *loaded_specs),
        scratch_shapes=[*load_scratch, *load_sems],
        compiler_params=params,
        cost_estimate=cost(1),
        name="late_terms",
    )(*tables, in_vmem(masked), in_smem(classes))
    pair = lax.ppermute(copied, "blk", same_chip)
    even_total, even_left, even_right, even_target, even_place, even_pair, even_next = even
    odd_total, odd_left, odd_right, odd_target, odd_place, odd_pair, odd_next = odd
    envs = tuple(in_vmem(x) for x in (even_left, even_right, odd_left, odd_right))
    even_total, odd_total = pl.pallas_call(
        pair_kernel,
        out_shape=(sums, sums),
        in_specs=[SMEM] * 6 + [VMEM] * 7,
        out_specs=(VMEM,) * 2,
        input_output_aliases={7: 0, 8: 1},
        compiler_params=params,
        cost_estimate=cost(0.001),
        name="pair_terms",
    )(
        *(in_smem(x) for x in (even_target, even_place, even_pair)),
        *(in_smem(x) for x in (odd_target, odd_place, odd_pair)),
        *(in_vmem(x) for x in (pair, even_total, odd_total)),
        *envs,
    )
    parts, _, _ = pl.pallas_call(
        next_kernel,
        out_shape=(pltpu.VMEM((groups, sectors, part_rows, size), jnp.bfloat16), sums, sums),
        in_specs=[SMEM] * 6 + [VMEM] * 7,
        out_specs=(VMEM,) * 3,
        input_output_aliases={7: 1, 8: 2},
        compiler_params=params,
        cost_estimate=cost(0.5),
        name="next_terms",
    )(
        *(in_smem(x) for x in (even_target, even_place, even_next)),
        *(in_smem(x) for x in (odd_target, odd_place, odd_next)),
        *(in_vmem(x) for x in (following, even_total, odd_total)),
        *envs,
    )
    received = lax.all_to_all(parts, "mpo", 0, 0)
    summed = received[0].astype(jnp.float32)
    for g in range(1, groups):
        summed += received[g].astype(jnp.float32)
    return jnp.where(keep != 0, summed, 0.0)


def solution(mesh):
    placed = (
        P("blk", None, None),
        P("blk"),
        P(("blk", "mpo"), None, None),
        P(("blk", "mpo"), None, None),
        P(("blk", "mpo")),
        P(("blk", "mpo")),
    )
    return jax.shard_map(
        body, mesh=mesh, in_specs=placed, out_specs=P("blk", "mpo", None), check_vma=False
    )
```

time: 37.6 us -> 37 us (0.984)
  waiting for transfers between devices: 4.55 us -> 3.97 us
  blocking collectives: 12.7 us -> 12.2 us
  starting transfers between devices: 13.6 us -> 14.1 us
    ppermute x1, waiting for transfers between devices: 4.55 us -> 2.09 us  [body(): following = lax.ppermute(masked, 'blk', next_chip)]
    ppermute x1, waiting for transfers between devices: 0.01 us -> 1.88 us  [body(): pair = lax.ppermute(copied, 'blk', same_chip)]
    ppermute x1, starting transfers between devices: 11.7 us -> 12.2 us  [body(): following = lax.ppermute(masked, 'blk', next_chip)]
    all_to_all x1, blocking collectives: 12.7 us -> 12.2 us  [body(): received = lax.all_to_all(parts, 'mpo', 0, 0)]
    pallas_call x2 -> x4, Pallas kernels: 5.44 us -> 5.63 us  [the longest x1 2.67 us: body(): pl.pallas_call(early_kernel, out_shape=(sent_rows, *loaded), in_specs=[AN...]
  transfers between devices with their start and end apart: 2 -> 2, of which waited for: 1 -> 2; matrix products, arithmetic and copies ran while one was open for 0% -> 0% of each run, Pallas kernels for 1% -> 3%
where the time goes in v4:
time: 37 us; the launch traced here: 36.8 us
  starting transfers between devices  14.1 us (38%)
  blocking collectives  12.2 us (33%)
  Pallas kernels  5.73 us (15%)
  waiting for transfers between devices  3.97 us (11%)
  other arithmetic  0.79 us (2%)
    ppermute x1, starting transfers between devices, body(): following = lax.ppermute(masked, 'blk', next_chip)  12.2 us
    all_to_all x1, blocking collectives, body(): received = lax.all_to_all(parts, 'mpo', 0, 0)  12.2 us
    pallas_call x1, Pallas kernels, body(): pl.pallas_call(early_kernel, out_shape=(sent_rows, *loaded), in_specs=[AN...  2.67 us
    ppermute x1, waiting for transfers between devices, body(): following = lax.ppermute(masked, 'blk', next_chip)  2.09 us
    ppermute x1, starting transfers between devices, body(): pair = lax.ppermute(copied, 'blk', same_chip)  1.92 us
    ppermute x1, waiting for transfers between devices, body(): pair = lax.ppermute(copied, 'blk', same_chip)  1.88 us
    pallas_call x1, Pallas kernels, body(): pl.pallas_call(mask_kernel, out_shape=(sent_rows, pltpu.SMEM((sectors,),...  1.14 us
    pallas_call x1, Pallas kernels, body(): pl.pallas_call(pair_kernel, out_shape=(sums, sums), in_specs=[SMEM] * 6 +...  0.93 us
  transfers between devices with their start and end apart: 2, of which 2 were waited for; matrix products, arithmetic and copies ran while one was open for 0% of the time, Pallas kernels for 3%

profile of v4, /device:TPU:56, one launch (start us, length us, event | category | flops | bytes accessed | tf_op | source)
XLA Modules:
  0.0 36.8 jit_solution(9357454956530468299)
XLA Ops:
  0.0 1.1 %masked.1 = (bf16[1040,256]{1,0:T(8,128)(2,1)S(1)}, s32[4]{0:T(128)S(4)}) custom-call(s32[4]{0:T(128)} %class_hbm.1, bf16[4,256,256]{2,1,0:T(8,128)(2,1)} %psi_hbm.1), custom_call_target="tpu_custom_call" | custom-call | tf_op jit(solution)/shard_map/masked/pallas_call | solution.py:266
  1.1 2.7 %early_terms.1 = (bf16[1040,256]{1,0:T(8,128)(2,1)S(1)}, f32[5,256,256]{2,1,0:T(8,128)S(1)}, bf16[16,256,256]{2,1,0:T(8,128)(2,1)S(1)}, bf16[16,256,256]{2,1,0:T...) custom-call(s32[16]{0:T(128)} %source_hbm.3, ...), custom_call_target="tpu_custom_call", output_to_operand_aliasing={{0}: (4, {})} | custom-call | tf_op jit(solution)/shard_map/early_terms/pallas_call | solution.py:275
  3.8 12.2 %collective-permute-start = (bf16[1040,256]{1,0:T(8,128)(2,1)S(1)}, bf16[1040,256]{1,0:T(8,128)(2,1)S(1)}, u32[]{:S(2)}, u32[]{:S(2)}) collective-permute-start(bf16[1040,256]{1,0:T(8,128)(2,1)S(1)} %get-tuple-element.28.own_ref), channel_id=1, source_target_pairs={{4,8},{8,4},{12,16},{16,12},{20,24},{24,20},{28,32},{32,28},{36,40... | collective-permute-start | bytes 1597448 | tf_op jit(solution)/shard_map/ppermute | solution.py:285
  16.0 0.1 late_terms.1
  16.1 1.9 %collective-permute-start.1 = (bf16[4,256,256]{2,1,0:T(8,128)(2,1)S(1)}, bf16[4,256,256]{2,1,0:T(8,128)(2,1)S(1)}, u32[]{:S(2)}, u32[]{:S(2)}) collective-permute-start(bf16[4,256,256]{2,1,0:T(8,128)(2,1)S(1)} %get-tuple-element.39), channel_id=1, source_target_pairs={{0,4},{4,0},{8,12},{12,8},{16,20},{20,16},{24,28},{28,24},{32,36},... | collective-permute-start | bytes 1572872 | tf_op jit(solution)/shard_map/ppermute | solution.py:296
  18.1 1.9 %collective-permute-done.1.pair_ref = bf16[4,256,256]{2,1,0:T(8,128)(2,1)S(1)} collective-permute-done((bf16[4,256,256]{2,1,0:T(8,128)(2,1)S(1)}, bf16[4,256,256]{2,1,0:T(8,128)(2,1)S(1)}, u32[]{:S(2)}, u32[]{:S(2)}) %collective-permute-start.1) | collective-permute-done | bytes 524320 | tf_op jit(solution)/shard_map/ppermute | solution.py:296
  19.9 0.9 %pair_terms.1 = (f32[5,256,256]{2,1,0:T(8,128)S(1)}, f32[5,256,256]{2,1,0:T(8,128)S(1)}) custom-call(s32[16]{0:T(128)S(4)} %get-tuple-element.31.even_target, s32[16]{0:T(128)S(4)} %get-tuple-element.32.even_place, s32[17]{0:T(128)S(4)} %get-tuple-element.37.even_queue, ...), custom_call_target="tpu_custom_call", output_to_operand_aliasing={{0}: (7, {}), {1}: (8, {})} | custom-call | flops 1073741 | bytes 4194 | tf_op jit(solution)/shard_map/pair_terms/pallas_call | solution.py:300
  20.9 2.1 %collective-permute-done.next_ref = bf16[1040,256]{1,0:T(8,128)(2,1)S(1)} collective-permute-done((bf16[1040,256]{1,0:T(8,128)(2,1)S(1)}, bf16[1040,256]{1,0:T(8,128)(2,1)S(1)}, u32[]{:S(2)}, u32[]{:S(2)}) %collective-permute-start) | collective-permute-done | bytes 532512 | tf_op jit(solution)/shard_map/ppermute | solution.py:285
  23.0 0.9 %next_terms.1 = (bf16[4,4,64,256]{3,2,1,0:T(8,128)(2,1)S(1)}, f32[5,256,256]{2,1,0:T(8,128)S(1)}, f32[5,256,256]{2,1,0:T(8,128)S(1)}) custom-call(s32[16]{0:T(128)S(4)} %get-tuple-element.31.even_target, s32[16]{0:T(128)S(4)} %get-tuple-element.32.even_place, s32[17]{0:T(128)S(4)} %get-tuple-element.33.even_queue, ...), custom_call_target="tpu_custom_call", output_to_operand_aliasing={{1}: (7, {}), {2}: (8, {})} | custom-call | flops 536870912 | bytes 2097152 | tf_op jit(solution)/shard_map/next_terms/pallas_call | solution.py:315
  23.9 12.2 %all_to_all.5 = bf16[4,4,64,256]{3,2,1,0:T(8,128)(2,1)S(1)} all-to-all(bf16[4,4,64,256]{3,2,1,0:T(8,128)(2,1)S(1)} %get-tuple-element.48), channel_id=1, replica_groups=mesh['blk'=192,'mpo'=4] {'mpo'}, dimensions={0} | all-to-all | bytes 1048576 | tf_op jit(solution)/shard_map/all_to_all | solution.py:330
  36.1 0.8 %bitcast_select_fusion = f32[4,64,256]{2,1,0:T(8,128)} fusion(f32[4,64,256]{2,1,0:T(8,128)S(1)} %get-tuple-element.30, bf16[4,4,64,256]{3,2,1,0:T(8,128)(2,1)S(1)} %all_to_all.5), kind=kLoop, calls=%fused_computation | loop fusion | flops 589824 | bytes 1048576 | tf_op jit(solution)/shard_map/jit(_where)/select_n | solution.py:334
Async XLA Ops:
  3.8 19.1 %collective-permute-start = (bf16[1040,256]{1,0:T(8,128)(2,1)S(1)}, bf16[1040,256]{1,0:T(8,128)(2,1)S(1)}, u32[]{:S(2)}, u32[]{:S(2)}) collective-permute-start(bf16[1040,256]{1,0:T(8,128)(2,1)S(1)} %get-tuple-element.28.own_ref), channel_id=1, source_target_pairs={{4,8},{8,4},{12,16},{16,12},{20,24},{24,20},{28,32},{32,28},{36,40... | collective-permute-start | bytes 1597448 | tf_op jit(solution)/shard_map/ppermute | solution.py:285
  16.1 3.8 %collective-permute-start.1 = (bf16[4,256,256]{2,1,0:T(8,128)(2,1)S(1)}, bf16[4,256,256]{2,1,0:T(8,128)(2,1)S(1)}, u32[]{:S(2)}, u32[]{:S(2)}) collective-permute-start(bf16[4,256,256]{2,1,0:T(8,128)(2,1)S(1)} %get-tuple-element.39), channel_id=1, source_target_pairs={{0,4},{4,0},{8,12},{12,8},{16,20},{20,16},{24,28},{28,24},{32,36},... | collective-permute-start | bytes 1572872 | tf_op jit(solution)/shard_map/ppermute | solution.py:296

commit v5 on v4

--- a/solution.py
+++ b/solution.py
@@ -70,18 +70,18 @@
         total[jnp.where(n < count, target_ref[t], sectors)] += term
 
 
-def add_terms(queue, block_of, target_ref, left_ref, right_ref, total, first=0):
+def add_terms(queue, block_of, target_ref, left_ref, right_ref, total, first=0, together=TOGETHER):
     refs = (queue, block_of, target_ref, left_ref, right_ref, total)
     count = queue[queue.shape[0] - 1]
     if first:
         add_together(0, first, *refs)
 
     def step(i, carry):
-        add_together(first + i * TOGETHER, TOGETHER, *refs)
+        add_together(first + i * together, together, *refs)
         return carry
 
     rest = jnp.maximum(count - first, 0)
-    lax.fori_loop(0, (rest + TOGETHER - 1) // TOGETHER, step, 0)
+    lax.fori_loop(0, (rest + together - 1) // together, step, 0)
 
 
 def load_terms(
@@ -215,7 +215,7 @@
         def block_of(t):
             return next_ref[pl.ds(pl.multiple_of(place_ref[t] * size, size), size), :]
 
-        add_terms(queue, block_of, target_ref, left_ref, right_ref, total, 8)
+        add_terms(queue, block_of, target_ref, left_ref, right_ref, total, 6, 2)
         for g in range(groups):
             for s in range(sectors):
                 parts_ref[g, s] = total[s, g * part_rows : (g + 1) * part_rows, :].astype(

time: 37 us -> 36.9 us (level)
  Pallas kernels: 5.73 us -> 5.08 us
  waiting for transfers between devices: 3.97 us -> 4.43 us
    pallas_call x1, Pallas kernels: 0.93 us -> 0.47 us  [body(): pl.pallas_call(pair_kernel, out_shape=(sums, sums), in_specs=[SMEM] * 6 +...]
    ppermute x1, waiting for transfers between devices: 2.09 us -> 2.56 us  [body(): following = lax.ppermute(masked, 'blk', next_chip)]
  transfers between devices with their start and end apart: 2 -> 2, of which waited for: 2 -> 2; matrix products, arithmetic and copies ran while one was open for 0% -> 0% of each run, Pallas kernels for 3% -> 2%
where the time goes in v5:
time: 36.9 us; the launch traced here: 36.7 us
  starting transfers between devices  14.1 us (38%)
  blocking collectives  12.2 us (33%)
  Pallas kernels  5.08 us (14%)
  waiting for transfers between devices  4.43 us (12%)
  other arithmetic  0.79 us (2%)
    ppermute x1, starting transfers between devices, body(): following = lax.ppermute(masked, 'blk', next_chip)  12.2 us
    all_to_all x1, blocking collectives, body(): received = lax.all_to_all(parts, 'mpo', 0, 0)  12.2 us
    pallas_call x1, Pallas kernels, body(): pl.pallas_call(early_kernel, out_shape=(sent_rows, *loaded), in_specs=[AN...  2.67 us
    ppermute x1, waiting for transfers between devices, body(): following = lax.ppermute(masked, 'blk', next_chip)  2.56 us
    ppermute x1, starting transfers between devices, body(): pair = lax.ppermute(copied, 'blk', same_chip)  1.92 us
    ppermute x1, waiting for transfers between devices, body(): pair = lax.ppermute(copied, 'blk', same_chip)  1.88 us
    pallas_call x1, Pallas kernels, body(): pl.pallas_call(mask_kernel, out_shape=(sent_rows, pltpu.SMEM((sectors,),...  1.14 us
    select_n x1, other arithmetic, body(): return jnp.where(keep != 0, summed, 0.0)  0.79 us
  transfers between devices with their start and end apart: 2, of which 2 were waited for; matrix products, arithmetic and copies ran while one was open for 0% of the time, Pallas kernels for 2%

profile of v5, /device:TPU:56, one launch (start us, length us, event | category | flops | bytes accessed | tf_op | source)
XLA Modules:
  0.0 36.7 jit_solution(1116309396229968963)
XLA Ops:
  0.0 1.1 %masked.1 = (bf16[1040,256]{1,0:T(8,128)(2,1)S(1)}, s32[4]{0:T(128)S(4)}) custom-call(s32[4]{0:T(128)} %class_hbm.1, bf16[4,256,256]{2,1,0:T(8,128)(2,1)} %psi_hbm.1), custom_call_target="tpu_custom_call" | custom-call | tf_op jit(solution)/shard_map/masked/pallas_call | solution.py:266
  1.1 2.7 %early_terms.1 = (bf16[1040,256]{1,0:T(8,128)(2,1)S(1)}, f32[5,256,256]{2,1,0:T(8,128)S(1)}, bf16[16,256,256]{2,1,0:T(8,128)(2,1)S(1)}, bf16[16,256,256]{2,1,0:T...) custom-call(s32[16]{0:T(128)} %source_hbm.3, ...), custom_call_target="tpu_custom_call", output_to_operand_aliasing={{0}: (4, {})} | custom-call | tf_op jit(solution)/shard_map/early_terms/pallas_call | solution.py:275
  3.8 12.2 %collective-permute-start = (bf16[1040,256]{1,0:T(8,128)(2,1)S(1)}, bf16[1040,256]{1,0:T(8,128)(2,1)S(1)}, u32[]{:S(2)}, u32[]{:S(2)}) collective-permute-start(bf16[1040,256]{1,0:T(8,128)(2,1)S(1)} %get-tuple-element.28.own_ref), channel_id=1, source_target_pairs={{4,8},{8,4},{12,16},{16,12},{20,24},{24,20},{28,32},{32,28},{36,40... | collective-permute-start | bytes 1597448 | tf_op jit(solution)/shard_map/ppermute | solution.py:285
  16.0 0.1 late_terms.1
  16.1 1.9 %collective-permute-start.1 = (bf16[4,256,256]{2,1,0:T(8,128)(2,1)S(1)}, bf16[4,256,256]{2,1,0:T(8,128)(2,1)S(1)}, u32[]{:S(2)}, u32[]{:S(2)}) collective-permute-start(bf16[4,256,256]{2,1,0:T(8,128)(2,1)S(1)} %get-tuple-element.39), channel_id=1, source_target_pairs={{0,4},{4,0},{8,12},{12,8},{16,20},{20,16},{24,28},{28,24},{32,36},... | collective-permute-start | bytes 1572872 | tf_op jit(solution)/shard_map/ppermute | solution.py:296
  18.1 1.9 %collective-permute-done.1.pair_ref = bf16[4,256,256]{2,1,0:T(8,128)(2,1)S(1)} collective-permute-done((bf16[4,256,256]{2,1,0:T(8,128)(2,1)S(1)}, bf16[4,256,256]{2,1,0:T(8,128)(2,1)S(1)}, u32[]{:S(2)}, u32[]{:S(2)}) %collective-permute-start.1) | collective-permute-done | bytes 524320 | tf_op jit(solution)/shard_map/ppermute | solution.py:296
  19.9 0.5 %pair_terms.1 = (f32[5,256,256]{2,1,0:T(8,128)S(1)}, f32[5,256,256]{2,1,0:T(8,128)S(1)}) custom-call(s32[16]{0:T(128)S(4)} %get-tuple-element.31.even_target, s32[16]{0:T(128)S(4)} %get-tuple-element.32.even_place, s32[17]{0:T(128)S(4)} %get-tuple-element.37.even_queue, ...), custom_call_target="tpu_custom_call", output_to_operand_aliasing={{0}: (7, {}), {1}: (8, {})} | custom-call | flops 1073741 | bytes 4194 | tf_op jit(solution)/shard_map/pair_terms/pallas_call | solution.py:300
  20.4 2.6 %collective-permute-done.next_ref = bf16[1040,256]{1,0:T(8,128)(2,1)S(1)} collective-permute-done((bf16[1040,256]{1,0:T(8,128)(2,1)S(1)}, bf16[1040,256]{1,0:T(8,128)(2,1)S(1)}, u32[]{:S(2)}, u32[]{:S(2)}) %collective-permute-start) | collective-permute-done | bytes 532512 | tf_op jit(solution)/shard_map/ppermute | solution.py:285
  23.0 0.7 %next_terms.1 = (bf16[4,4,64,256]{3,2,1,0:T(8,128)(2,1)S(1)}, f32[5,256,256]{2,1,0:T(8,128)S(1)}, f32[5,256,256]{2,1,0:T(8,128)S(1)}) custom-call(s32[16]{0:T(128)S(4)} %get-tuple-element.31.even_target, s32[16]{0:T(128)S(4)} %get-tuple-element.32.even_place, s32[17]{0:T(128)S(4)} %get-tuple-element.33.even_queue, ...), custom_call_target="tpu_custom_call", output_to_operand_aliasing={{1}: (7, {}), {2}: (8, {})} | custom-call | flops 536870912 | bytes 2097152 | tf_op jit(solution)/shard_map/next_terms/pallas_call | solution.py:315
  23.7 12.2 %all_to_all.5 = bf16[4,4,64,256]{3,2,1,0:T(8,128)(2,1)S(1)} all-to-all(bf16[4,4,64,256]{3,2,1,0:T(8,128)(2,1)S(1)} %get-tuple-element.48), channel_id=1, replica_groups=mesh['blk'=192,'mpo'=4] {'mpo'}, dimensions={0} | all-to-all | bytes 1048576 | tf_op jit(solution)/shard_map/all_to_all | solution.py:330
  35.9 0.8 %bitcast_select_fusion = f32[4,64,256]{2,1,0:T(8,128)} fusion(f32[4,64,256]{2,1,0:T(8,128)S(1)} %get-tuple-element.30, bf16[4,4,64,256]{3,2,1,0:T(8,128)(2,1)S(1)} %all_to_all.5), kind=kLoop, calls=%fused_computation | loop fusion | flops 589824 | bytes 1048576 | tf_op jit(solution)/shard_map/jit(_where)/select_n | solution.py:334
Async XLA Ops:
  3.8 19.1 %collective-permute-start = (bf16[1040,256]{1,0:T(8,128)(2,1)S(1)}, bf16[1040,256]{1,0:T(8,128)(2,1)S(1)}, u32[]{:S(2)}, u32[]{:S(2)}) collective-permute-start(bf16[1040,256]{1,0:T(8,128)(2,1)S(1)} %get-tuple-element.28.own_ref), channel_id=1, source_target_pairs={{4,8},{8,4},{12,16},{16,12},{20,24},{24,20},{28,32},{32,28},{36,40... | collective-permute-start | bytes 1597448 | tf_op jit(solution)/shard_map/ppermute | solution.py:285
  16.1 3.8 %collective-permute-start.1 = (bf16[4,256,256]{2,1,0:T(8,128)(2,1)S(1)}, bf16[4,256,256]{2,1,0:T(8,128)(2,1)S(1)}, u32[]{:S(2)}, u32[]{:S(2)}) collective-permute-start(bf16[4,256,256]{2,1,0:T(8,128)(2,1)S(1)} %get-tuple-element.39), channel_id=1, source_target_pairs={{0,4},{4,0},{8,12},{12,8},{16,20},{20,16},{24,28},{28,24},{32,36},... | collective-permute-start | bytes 1572872 | tf_op jit(solution)/shard_map/ppermute | solution.py:296

commit v6 on v5

--- a/solution.py
+++ b/solution.py
@@ -215,7 +215,7 @@
         def block_of(t):
             return next_ref[pl.ds(pl.multiple_of(place_ref[t] * size, size), size), :]
 
-        add_terms(queue, block_of, target_ref, left_ref, right_ref, total, 6, 2)
+        add_terms(queue, block_of, target_ref, left_ref, right_ref, total, 7, 3)
         for g in range(groups):
             for s in range(sectors):
                 parts_ref[g, s] = total[s, g * part_rows : (g + 1) * part_rows, :].astype(

time: 36.9 us -> 36.9 us (level)
  no operation moved by 1% of the time
where the time goes in v6:
time: 36.9 us; the launch traced here: 36.7 us
  starting transfers between devices  14.1 us (38%)
  blocking collectives  12.2 us (33%)
  Pallas kernels  5.14 us (14%)
  waiting for transfers between devices  4.43 us (12%)
  other arithmetic  0.79 us (2%)
    ppermute x1, starting transfers between devices, body(): following = lax.ppermute(masked, 'blk', next_chip)  12.2 us
    all_to_all x1, blocking collectives, body(): received = lax.all_to_all(parts, 'mpo', 0, 0)  12.2 us
    pallas_call x1, Pallas kernels, body(): pl.pallas_call(early_kernel, out_shape=(sent_rows, *loaded), in_specs=[AN...  2.67 us
    ppermute x1, waiting for transfers between devices, body(): following = lax.ppermute(masked, 'blk', next_chip)  2.56 us
    ppermute x1, starting transfers between devices, body(): pair = lax.ppermute(copied, 'blk', same_chip)  1.92 us
    ppermute x1, waiting for transfers between devices, body(): pair = lax.ppermute(copied, 'blk', same_chip)  1.88 us
    pallas_call x1, Pallas kernels, body(): pl.pallas_call(mask_kernel, out_shape=(sent_rows, pltpu.SMEM((sectors,),...  1.14 us
    select_n x1, other arithmetic, body(): return jnp.where(keep != 0, summed, 0.0)  0.79 us
  transfers between devices with their start and end apart: 2, of which 2 were waited for; matrix products, arithmetic and copies ran while one was open for 0% of the time, Pallas kernels for 2%

profile of v6, /device:TPU:56, one launch (start us, length us, event | category | flops | bytes accessed | tf_op | source)
XLA Modules:
  0.0 36.7 jit_solution(17172857727196745576)
XLA Ops:
  0.0 1.1 %masked.1 = (bf16[1040,256]{1,0:T(8,128)(2,1)S(1)}, s32[4]{0:T(128)S(4)}) custom-call(s32[4]{0:T(128)} %class_hbm.1, bf16[4,256,256]{2,1,0:T(8,128)(2,1)} %psi_hbm.1), custom_call_target="tpu_custom_call" | custom-call | tf_op jit(solution)/shard_map/masked/pallas_call | solution.py:266
  1.1 2.7 %early_terms.1 = (bf16[1040,256]{1,0:T(8,128)(2,1)S(1)}, f32[5,256,256]{2,1,0:T(8,128)S(1)}, bf16[16,256,256]{2,1,0:T(8,128)(2,1)S(1)}, bf16[16,256,256]{2,1,0:T...) custom-call(s32[16]{0:T(128)} %source_hbm.3, ...), custom_call_target="tpu_custom_call", output_to_operand_aliasing={{0}: (4, {})} | custom-call | tf_op jit(solution)/shard_map/early_terms/pallas_call | solution.py:275
  3.8 12.2 %collective-permute-start = (bf16[1040,256]{1,0:T(8,128)(2,1)S(1)}, bf16[1040,256]{1,0:T(8,128)(2,1)S(1)}, u32[]{:S(2)}, u32[]{:S(2)}) collective-permute-start(bf16[1040,256]{1,0:T(8,128)(2,1)S(1)} %get-tuple-element.28.own_ref), channel_id=1, source_target_pairs={{4,8},{8,4},{12,16},{16,12},{20,24},{24,20},{28,32},{32,28},{36,40... | collective-permute-start | bytes 1597448 | tf_op jit(solution)/shard_map/ppermute | solution.py:285
  16.0 0.1 late_terms.1
  16.1 1.9 %collective-permute-start.1 = (bf16[4,256,256]{2,1,0:T(8,128)(2,1)S(1)}, bf16[4,256,256]{2,1,0:T(8,128)(2,1)S(1)}, u32[]{:S(2)}, u32[]{:S(2)}) collective-permute-start(bf16[4,256,256]{2,1,0:T(8,128)(2,1)S(1)} %get-tuple-element.39), channel_id=1, source_target_pairs={{0,4},{4,0},{8,12},{12,8},{16,20},{20,16},{24,28},{28,24},{32,36},... | collective-permute-start | bytes 1572872 | tf_op jit(solution)/shard_map/ppermute | solution.py:296
  18.1 1.9 %collective-permute-done.1.pair_ref = bf16[4,256,256]{2,1,0:T(8,128)(2,1)S(1)} collective-permute-done((bf16[4,256,256]{2,1,0:T(8,128)(2,1)S(1)}, bf16[4,256,256]{2,1,0:T(8,128)(2,1)S(1)}, u32[]{:S(2)}, u32[]{:S(2)}) %collective-permute-start.1) | collective-permute-done | bytes 524320 | tf_op jit(solution)/shard_map/ppermute | solution.py:296
  19.9 0.5 %pair_terms.1 = (f32[5,256,256]{2,1,0:T(8,128)S(1)}, f32[5,256,256]{2,1,0:T(8,128)S(1)}) custom-call(s32[16]{0:T(128)S(4)} %get-tuple-element.31.even_target, s32[16]{0:T(128)S(4)} %get-tuple-element.32.even_place, s32[17]{0:T(128)S(4)} %get-tuple-element.37.even_queue, ...), custom_call_target="tpu_custom_call", output_to_operand_aliasing={{0}: (7, {}), {1}: (8, {})} | custom-call | flops 1073741 | bytes 4194 | tf_op jit(solution)/shard_map/pair_terms/pallas_call | solution.py:300
  20.4 2.6 %collective-permute-done.next_ref = bf16[1040,256]{1,0:T(8,128)(2,1)S(1)} collective-permute-done((bf16[1040,256]{1,0:T(8,128)(2,1)S(1)}, bf16[1040,256]{1,0:T(8,128)(2,1)S(1)}, u32[]{:S(2)}, u32[]{:S(2)}) %collective-permute-start) | collective-permute-done | bytes 532512 | tf_op jit(solution)/shard_map/ppermute | solution.py:285
  23.0 0.8 %next_terms.1 = (bf16[4,4,64,256]{3,2,1,0:T(8,128)(2,1)S(1)}, f32[5,256,256]{2,1,0:T(8,128)S(1)}, f32[5,256,256]{2,1,0:T(8,128)S(1)}) custom-call(s32[16]{0:T(128)S(4)} %get-tuple-element.31.even_target, s32[16]{0:T(128)S(4)} %get-tuple-element.32.even_place, s32[17]{0:T(128)S(4)} %get-tuple-element.33.even_queue, ...), custom_call_target="tpu_custom_call", output_to_operand_aliasing={{1}: (7, {}), {2}: (8, {})} | custom-call | flops 536870912 | bytes 2097152 | tf_op jit(solution)/shard_map/next_terms/pallas_call | solution.py:315
  23.8 12.2 %all_to_all.5 = bf16[4,4,64,256]{3,2,1,0:T(8,128)(2,1)S(1)} all-to-all(bf16[4,4,64,256]{3,2,1,0:T(8,128)(2,1)S(1)} %get-tuple-element.48), channel_id=1, replica_groups=mesh['blk'=192,'mpo'=4] {'mpo'}, dimensions={0} | all-to-all | bytes 1048576 | tf_op jit(solution)/shard_map/all_to_all | solution.py:330
  35.9 0.8 %bitcast_select_fusion = f32[4,64,256]{2,1,0:T(8,128)} fusion(f32[4,64,256]{2,1,0:T(8,128)S(1)} %get-tuple-element.30, bf16[4,4,64,256]{3,2,1,0:T(8,128)(2,1)S(1)} %all_to_all.5), kind=kLoop, calls=%fused_computation | loop fusion | flops 589824 | bytes 1048576 | tf_op jit(solution)/shard_map/jit(_where)/select_n | solution.py:334
Async XLA Ops:
  3.8 19.1 %collective-permute-start = (bf16[1040,256]{1,0:T(8,128)(2,1)S(1)}, bf16[1040,256]{1,0:T(8,128)(2,1)S(1)}, u32[]{:S(2)}, u32[]{:S(2)}) collective-permute-start(bf16[1040,256]{1,0:T(8,128)(2,1)S(1)} %get-tuple-element.28.own_ref), channel_id=1, source_target_pairs={{4,8},{8,4},{12,16},{16,12},{20,24},{24,20},{28,32},{32,28},{36,40... | collective-permute-start | bytes 1597448 | tf_op jit(solution)/shard_map/ppermute | solution.py:285
  16.1 3.8 %collective-permute-start.1 = (bf16[4,256,256]{2,1,0:T(8,128)(2,1)S(1)}, bf16[4,256,256]{2,1,0:T(8,128)(2,1)S(1)}, u32[]{:S(2)}, u32[]{:S(2)}) collective-permute-start(bf16[4,256,256]{2,1,0:T(8,128)(2,1)S(1)} %get-tuple-element.39), channel_id=1, source_target_pairs={{0,4},{4,0},{8,12},{12,8},{16,20},{20,16},{24,28},{28,24},{32,36},... | collective-permute-start | bytes 1572872 | tf_op jit(solution)/shard_map/ppermute | solution.py:296
